TPU v7x, 32 devices: a whole 2x2x4 slice. The times are simulated.
32 devices in a mesh: basin: 2 (over y), tx: 4 (over z), ty: 2 (over core), ev: 2 (over x).
Axes of the slice: x: 2, y: 2, z: 4, core: 2. Of those that a mesh axis runs over, the one named last changes fastest.
Arguments:
- depth0: float32 [4, 8, 8, 8, 256], P(('basin', 'ev'), None, None, 'tx', 'ty'), parts along dimension 0, may hold values from 0.6 to 1.4
- momentum0: float32 [4, 2, 8, 8, 8, 256], P(('basin', 'ev'), None, None, None, 'tx', 'ty'), parts along dimension 0, may hold values from -2.5 to 2.5
- obs_weight: float32 [4, 8, 8, 8, 256], P(('basin', 'ev'), None, None, 'tx', 'ty'), parts along dimension 0, as said below
- wet_mask: int32 [4, 4, 8, 256], P(('basin', 'ev'), None, 'tx', 'ty'), parts along dimension 0, may hold values 0 or 1
- zone_id: int32 [16, 256], P(('basin', 'tx'), 'ty'), parts along dimension 0, may hold values from 0 to 31
- manning: float32 [64], P('basin'), parts along dimension 0, may hold values from 0.2 to 0.6
Outputs:
- adjoint_state: float32 [4, 3, 8, 8, 8, 256], P(('basin', 'ev'), None, None, None, 'tx', 'ty'), parts along dimension 0
- rough_grad: float32 [64], P('basin'), parts along dimension 0
There are 2 independent parts, one for each index of `basin`. A program takes and returns all parts, laid end to end along the dimension named above; each array names one. Nothing has to cross between parts.
Inputs may be any that keep to these rules, and one draw needn't show every extreme that they name: `wet_mask`: 1 where an element is wet in that section of that event, else 0. `obs_weight`: positive weights.
All inputs are finite; a program needn't handle non-finite values. No bound on the sum of `wet_mask` on one device may be relied on, other than what follows from the above.
Results may differ from a plain program's by a relative error of at most 0.00005.
Values sent between devices are 32-bit elements; how exact they have to be, the bound alone decides.
A program may use at most 64 MiB of HBM per device.

v0:
```python
import functools

import jax
import jax.numpy as jnp
import numpy as np
from jax import lax
from jax.experimental import pallas as pl
from jax.experimental.pallas import tpu as pltpu
from jax.sharding import PartitionSpec as P

NP = 8
SECTIONS = 4
ZONES = 32
SUB = 8

PENALTY_SPEED = 4.0
TIME_STEP = 0.0005
SPEED_FLOOR = 0.01
MESH = pl.DeviceIdType.MESH
EAST, WEST, NORTH, SOUTH = range(4)


def node_tables():
    points = -np.cos(np.pi * np.arange(NP) / (NP - 1))
    identity = np.eye(NP)
    differ = points[:, None] - points[None, :] + identity
    barycentric = 1.0 / np.prod(differ, axis=1)
    derivative = barycentric[None, :] / barycentric[:, None] / differ * (1.0 - identity)
    derivative = derivative - identity * derivative.sum(axis=1)[:, None]
    order = NP - 1
    end_weight = 1.0 / (order * order)
    return (derivative, float(1.0 / end_weight))


def along_first(table, slabs):
    half = NP // 2
    even = [slabs[k] + slabs[NP - 1 - k] for k in range(half)]
    odd = [slabs[k] - slabs[NP - 1 - k] for k in range(half)]
    out = [None] * NP
    for a in range(half):
        on_even = sum(float(0.5 * (table[a, k] + table[a, NP - 1 - k])) * even[k] for k in range(half))
        on_odd = sum(float(0.5 * (table[a, k] - table[a, NP - 1 - k])) * odd[k] for k in range(half))
        out[a] = on_odd + on_even
        out[NP - 1 - a] = on_odd - on_even
    return out


def kernel(
    axes, ext_x, events,
    depth_ref, mom_ref, weight_ref, wet_ref, zone_ref, manning_ref,
    adj_ref, grad_ref,
    state, vel_x, vel_y, inv_h, drag_r, flux_x, flux_y, tend, acc, final_adj, later,
    wet_rows, rough_rows, coef_y, zone_acc,
    xs, xr, ys, yr, zs, zr, send_sem, recv_sem, zsend_sem, zrecv_sem,
):
    table, lift = node_tables()
    n_tx, n_ty, n_ev = axes["tx"], axes["ty"], axes["ev"]
    tx, ty, ev = lax.axis_index("tx"), lax.axis_index("ty"), lax.axis_index("ev")
    ext_y = depth_ref.shape[-1]
    groups = ext_x
    step = ext_x
    has = {EAST: tx < n_tx - 1, WEST: tx > 0, NORTH: ty < n_ty - 1, SOUTH: ty > 0}
    target = {EAST: {"tx": tx + 1}, WEST: {"tx": tx - 1}, NORTH: {"ty": ty + 1}, SOUTH: {"ty": ty - 1}}
    opposite = {EAST: WEST, WEST: EAST, NORTH: SOUTH, SOUTH: NORTH}

    plane = n_ty * n_ev
    here = ty * n_ev + ev
    barrier = pltpu.get_barrier_semaphore()
    plane_peers = []
    for k in range(1, plane):
        other = lax.rem(here + k, plane)
        plane_peers.append((k, {"ty": other // n_ev, "ev": lax.rem(other, n_ev)}))
    line_peers = [(k, {"tx": lax.rem(tx + k, n_tx)}) for k in range(1, n_tx)]
    for _, peer in plane_peers + line_peers:
        pl.semaphore_signal(barrier, inc=1, device_id=peer, device_id_type=MESH)

    sub = lax.broadcasted_iota(jnp.int32, (SUB, ext_y), 0)
    lane = lax.broadcasted_iota(jnp.int32, (SUB, ext_y), 1)
    elem = lax.rem(sub, ext_x)
    one = jnp.float32(1.0)

    def flag(yes):
        return jnp.where(yes, 1, 0)

    inside = {
        WEST: jnp.where((elem == 0) & (flag(has[WEST]) == 0), 0.0, one),
        EAST: jnp.where((elem == ext_x - 1) & (flag(has[EAST]) == 0), 0.0, one),
        SOUTH: jnp.where((sub >= ext_x) | ((lane == 0) & (flag(has[SOUTH]) == 0)), 0.0, one),
        NORTH: jnp.where((sub < SUB - ext_x) | ((lane == ext_y - 1) & (flag(has[NORTH]) == 0)), 0.0, one),
    }
    first_elem = (elem == 0) & (flag(has[WEST]) == 1)
    last_elem = (elem == ext_x - 1) & (flag(has[EAST]) == 1)
    first_lane = (lane == 0) & (flag(has[SOUTH]) == 1)
    last_lane = (lane == ext_y - 1) & (flag(has[NORTH]) == 1)

    def spread(rows):
        out = jnp.broadcast_to(rows[0:1], (SUB, ext_y))
        for e in range(1, ext_x):
            out = jnp.where(elem == e, jnp.broadcast_to(rows[e:e + 1], (SUB, ext_y)), out)
        return out

    for s in range(SECTIONS):
        wet_rows[s] = spread(wet_ref[s].astype(jnp.float32))
    zone = spread(zone_ref[...])
    rough = jnp.zeros((SUB, ext_y), jnp.float32)
    for z in range(ZONES):
        rough = jnp.where(zone == z, manning_ref[z], rough)
    rough_rows[...] = rough

    for t, mat in enumerate((table, table.T)):
        for g in range(groups):
            for h in range(groups):
                for k in range(SUB // step):
                    column = jnp.zeros((SUB, ext_y), jnp.float32)
                    for r in range(SUB):
                        a = (SUB * g + r) // ext_x
                        b = (SUB * h + (r - k * step) % SUB) // ext_x
                        column = jnp.where(sub == r, jnp.float32(-mat[a, b]), column)
                    coef_y[t, g, h, k] = column
    zone_acc[...] = jnp.zeros((SUB, ext_y), jnp.float32)

    def rows(g):
        return pl.ds(SUB * g, SUB)

    def roll(value, shift, axis):
        size = value.shape[axis]
        shift = shift % size
        return value if shift == 0 else pltpu.roll(value, shift, axis)

    def minus_along_second(t, source):
        turned = [[roll(source[h], k * step, 0) for k in range(SUB // step)] for h in range(groups)]
        return [
            sum(coef_y[t, g, h, k] * turned[h][k] for h in range(groups) for k in range(SUB // step))
            for g in range(groups)
        ]

    def copy(rnd, side):
        pair, slot = ((xs, xr), side) if side in (EAST, WEST) else ((ys, yr), side - 2)
        return pltpu.make_async_remote_copy(
            src_ref=pair[0].at[rnd, slot],
            dst_ref=pair[1].at[rnd, slot],
            send_sem=send_sem.at[rnd, side],
            recv_sem=recv_sem.at[rnd, side],
            device_id=target[side],
            device_id_type=MESH,
        )

    def start(rnd, sides):
        for side in sides:
            @pl.when(has[side])
            def _():
                copy(rnd, side).start()

    def await_all(rnd, sides):
        for side in sides:
            @pl.when(has[opposite[side]])
            def _():
                copy(rnd, side).wait_recv()

    def pack_x(rnd, c, east, west):
        to_east, to_west = east[0], west[0]
        for g in range(1, groups):
            to_east = jnp.where(elem == ext_x - 1 - g, roll(east[g], -g, 0), to_east)
            to_west = jnp.where(elem == g, roll(west[g], g, 0), to_west)
        xs[rnd, EAST, c] = to_east
        xs[rnd, WEST, c] = to_west

    def beside_x(rnd, c, g, east, west):
        from_west, from_east = xr[rnd, EAST, c], xr[rnd, WEST, c]
        at_west = jnp.where(first_elem, roll(from_west, -(ext_x - 1 - g), 0), roll(east[g], 1, 0))
        at_east = jnp.where(last_elem, roll(from_east, ext_x - 1 - g, 0), roll(west[g], -1, 0))
        return at_west, at_east

    def pack_y(rnd, c, i, north, south):
        ys[rnd, 0, c, i] = roll(roll(north, ext_x, 0), 1, 1)
        ys[rnd, 1, c, i] = roll(roll(south, -ext_x, 0), -1, 1)

    def beside_y(rnd, c, i):
        at_south = jnp.where(first_lane, yr[rnd, 0, c, i], ys[rnd, 0, c, i])
        at_north = jnp.where(last_lane, yr[rnd, 1, c, i], ys[rnd, 1, c, i])
        return at_south, at_north

    first, last = 0, groups - 1
    comps = range(3)
    pen = 0.5 * PENALTY_SPEED

    def put_fluxes(s, i):
        for g in range(groups):
            h, p, m = (state[s, c, i, rows(g)] for c in comps)
            ih = 1.0 / h
            u, v = p * ih, m * ih
            inv_h[s, i, rows(g)] = ih
            vel_x[s, i, rows(g)] = u
            vel_y[s, i, rows(g)] = v
            pressure = 0.5 * h * h
            cross = p * v
            fx = (p, p * u + pressure, cross)
            fy = (m, cross, m * v + pressure)
            for c, q in enumerate((h, p, m)):
                flux_x[c, i, rows(g)] = fx[c]
                flux_y[c, i, rows(g)] = fy[c]
            if g == last:
                for c, q in enumerate((h, p, m)):
                    ys[s, 0, c, i] = roll(roll(0.5 * fy[c] + pen * q, ext_x, 0), 1, 1)
            if g == first:
                for c, q in enumerate((h, p, m)):
                    ys[s, 1, c, i] = roll(roll(pen * q - 0.5 * fy[c], -ext_x, 0), -1, 1)

    def x_traces(s, c):
        east = [0.5 * flux_x[c, NP - 1, rows(g)] + pen * state[s, c, NP - 1, rows(g)] for g in range(groups)]
        west = [pen * state[s, c, 0, rows(g)] - 0.5 * flux_x[c, 0, rows(g)] for g in range(groups)]
        return east, west

    coefs = (0.5 * TIME_STEP, 0.5 * TIME_STEP, TIME_STEP)
    sums = (1.0, 2.0, 2.0, 1.0)
    final_weights = (TIME_STEP / 6.0, TIME_STEP / 3.0, TIME_STEP / 3.0, TIME_STEP / 6.0)

    def send_forward(s):
        for c in comps:
            pack_x(s, c, *x_traces(s, c))
        start(s, (EAST, WEST, NORTH, SOUTH))

    def set_up(i, _):
        state[0, 0, i] = depth_ref[i]
        state[0, 1, i] = mom_ref[0, i]
        state[0, 2, i] = mom_ref[1, i]
        put_fluxes(0, i)
        return _

    lax.fori_loop(0, NP, set_up, 0)
    pl.semaphore_wait(barrier, len(plane_peers) + len(line_peers))
    send_forward(0)

    for s in range(SECTIONS):
        def volume(i, _):
            for c in comps:
                out = minus_along_second(0, [flux_y[c, i, rows(g)] for g in range(groups)])
                for g in range(groups):
                    tend[c, i, rows(g)] = out[g]
            for g in range(groups):
                h, p, m = (state[s, c, i, rows(g)] for c in comps)
                u, v = vel_x[s, i, rows(g)], vel_y[s, i, rows(g)]
                speed = jnp.sqrt(u * u + v * v + SPEED_FLOOR)
                rough_g = rough_rows[...]
                kr = rough_g * speed * jnp.exp((-4.0 / 3.0) * jnp.log(h))
                drag_r[s, i, rows(g)] = kr
                k = rough_g * kr
                tend[1, i, rows(g)] -= k * p
                tend[2, i, rows(g)] -= k * m
            return _

        lax.fori_loop(0, NP, volume, 0)

        def volume_x(c, _):
            for g in range(groups):
                out = along_first(table, [flux_x[c, i, rows(g)] for i in range(NP)])
                for i in range(NP):
                    tend[c, i, rows(g)] -= out[i]
            return _

        lax.fori_loop(0, 3, volume_x, 0)

        await_all(s, (EAST, WEST, NORTH, SOUTH))
        for c in comps:
            east, west = x_traces(s, c)
            for g in range(groups):
                at_west, at_east = beside_x(s, c, g, east, west)
                q0, q7 = state[s, c, 0, rows(g)], state[s, c, NP - 1, rows(g)]
                f0, f7 = flux_x[c, 0, rows(g)], flux_x[c, NP - 1, rows(g)]
                tend[c, 0, rows(g)] += (lift * inside[WEST]) * (at_west - (0.5 * f0 + pen * q0))
                tend[c, NP - 1, rows(g)] += (lift * inside[EAST]) * (at_east - (pen * q7 - 0.5 * f7))

        def finish(i, _):
            wet = wet_rows[s]
            for c in comps:
                at_south, at_north = beside_y(s, c, i)
                own_s = 0.5 * flux_y[c, i, rows(first)] + pen * state[s, c, i, rows(first)]
                own_n = pen * state[s, c, i, rows(last)] - 0.5 * flux_y[c, i, rows(last)]
                for g in range(groups):
                    slope = tend[c, i, rows(g)]
                    if g == first:
                        slope = slope + (lift * inside[SOUTH]) * (at_south - own_s)
                    if g == last:
                        slope = slope + (lift * inside[NORTH]) * (at_north - own_n)
                    slope = wet * slope
                    start_q = state[0, c, i, rows(g)]
                    if s == 0:
                        acc[c, i, rows(g)] = slope
                    elif s < SECTIONS - 1:
                        acc[c, i, rows(g)] += sums[s] * slope
                    if s < SECTIONS - 1:
                        state[s + 1, c, i, rows(g)] = start_q + coefs[s] * slope
                    elif c > 0:
                        total = acc[c, i, rows(g)] + slope
                        final = start_q + (TIME_STEP / 6.0) * total
                        seed = weight_ref[i, rows(g)] * final
                        final_adj[c - 1, i, rows(g)] = seed
                        adj_ref[c, i, rows(g)] = seed
                    else:
                        adj_ref[c, i, rows(g)] = jnp.zeros((SUB, ext_y), jnp.float32)
            if s < SECTIONS - 1:
                put_fluxes(s + 1, i)
            else:
                put_cot(s, i)
            return _

        def put_cot(s, i):
            wet = wet_rows[s]
            for c in comps:
                cot = []
                for g in range(groups):
                    value = None
                    if c > 0:
                        value = final_weights[s] * final_adj[c - 1, i, rows(g)]
                    if s < SECTIONS - 1:
                        back = coefs[s] * later[c, i, rows(g)]
                        value = back if value is None else value + back
                    if value is None:
                        value = jnp.zeros((SUB, ext_y), jnp.float32)
                    value = wet * value
                    acc[c, i, rows(g)] = value
                    cot.append(value)
                pack_y(2 * SECTIONS - 1 - s, c, i, cot[last], cot[first])

        lax.fori_loop(0, NP, finish, 0)
        if s < SECTIONS - 1:
            send_forward(s + 1)

    def cot_faces(c):
        return (
            [acc[c, NP - 1, rows(g)] for g in range(groups)],
            [acc[c, 0, rows(g)] for g in range(groups)],
        )

    def plane_copy(k, peer):
        return pltpu.make_async_remote_copy(
            src_ref=zs.at[0], dst_ref=zr.at[k],
            send_sem=zsend_sem.at[k], recv_sem=zrecv_sem.at[k],
            device_id=peer, device_id_type=MESH,
        )

    def line_copy(k, peer):
        slot = plane + k
        return pltpu.make_async_remote_copy(
            src_ref=zs.at[1], dst_ref=zr.at[slot],
            send_sem=zsend_sem.at[slot], recv_sem=zrecv_sem.at[slot],
            device_id=peer, device_id_type=MESH,
        )

    for s in reversed(range(SECTIONS)):
        rnd = 2 * SECTIONS - 1 - s
        for c in comps:
            pack_x(rnd, c, *cot_faces(c))
        start(rnd, (EAST, WEST, NORTH, SOUTH))

        def drag_back(i, _):
            for g in range(groups):
                h, p, m = (state[s, c, i, rows(g)] for c in comps)
                u, v, ih = vel_x[s, i, rows(g)], vel_y[s, i, rows(g)], inv_h[s, i, rows(g)]
                kr = drag_r[s, i, rows(g)]
                c1, c2 = acc[1, i, rows(g)], acc[2, i, rows(g)]
                rough_g = rough_rows[...]
                dot = c1 * p + c2 * m
                part = kr * dot
                zone_acc[...] += part
                k = rough_g * kr
                e = rough_g * part * ih
                square = u * u + v * v
                q = 1.0 / (square + SPEED_FLOOR)
                eq = e * q
                tend[0, i, rows(g)] = (4.0 / 3.0) * e + eq * square
                tend[1, i, rows(g)] = -(k * c1 + eq * u)
                tend[2, i, rows(g)] = -(k * c2 + eq * v)
            return _

        lax.fori_loop(0, NP, drag_back, 0)

        if s == 0:
            total = zone_acc[...]
            shift = ext_x
            while shift < SUB:
                total = total + roll(total, shift, 0)
                shift *= 2
            total = -2.0 * total
            zones = lax.broadcasted_iota(jnp.int32, (ZONES, ext_y), 0)
            spot = jnp.zeros((ZONES, ext_y), jnp.float32)
            for e in range(ext_x):
                ids = jnp.broadcast_to(zone_ref[e:e + 1, :], (ZONES, ext_y))
                spot = spot + jnp.where(ids == zones, jnp.broadcast_to(total[e:e + 1], (ZONES, ext_y)), 0.0)
            per_zone = jnp.sum(spot, axis=1, keepdims=True)
            spots = lax.broadcasted_iota(jnp.int32, (ZONES, ext_y), 1)
            line = jnp.sum(jnp.where(zones == spots, jnp.broadcast_to(per_zone, (ZONES, ext_y)), 0.0), axis=0, keepdims=True)
            zs[0] = line
            for k, peer in plane_peers:
                plane_copy(k, peer).start()

        def volume_y(i, _):
            for c in comps:
                out = minus_along_second(1, [acc[c, i, rows(g)] for g in range(groups)])
                for g in range(groups):
                    flux_y[c, i, rows(g)] = out[g]
            return _

        lax.fori_loop(0, NP, volume_y, 0)

        def volume_back(c, _):
            for g in range(groups):
                out = along_first(-table.T, [acc[c, i, rows(g)] for i in range(NP)])
                for i in range(NP):
                    flux_x[c, i, rows(g)] = out[i]
            return _

        lax.fori_loop(0, 3, volume_back, 0)

        await_all(rnd, (EAST, WEST, NORTH, SOUTH))
        if s == 0:
            mine = zs[0]
            for k, peer in plane_peers:
                plane_copy(k, peer).wait_recv()
                mine = mine + zr[k]
            zs[1] = mine
            for k, peer in line_peers:
                line_copy(k, peer).start()
        for c in comps:
            east, west = cot_faces(c)
            for g in range(groups):
                at_west, at_east = beside_x(rnd, c, g, east, west)
                w_in, e_in = lift * inside[WEST], lift * inside[EAST]
                flux_x[c, 0, rows(g)] -= (0.5 * w_in) * (west[g] + at_west)
                tend[c, 0, rows(g)] += (pen * w_in) * (at_west - west[g])
                flux_x[c, NP - 1, rows(g)] += (0.5 * e_in) * (east[g] + at_east)
                tend[c, NP - 1, rows(g)] += (pen * e_in) * (at_east - east[g])

        def finish_back(i, _):
            s_in, n_in = lift * inside[SOUTH], lift * inside[NORTH]
            beside = [beside_y(rnd, c, i) for c in comps]
            for g in range(groups):
                a = [flux_x[c, i, rows(g)] for c in comps]
                b = [flux_y[c, i, rows(g)] for c in comps]
                out = [tend[c, i, rows(g)] for c in comps]
                own = [acc[c, i, rows(g)] for c in comps]
                for c in comps:
                    at_south, at_north = beside[c]
                    if g == first:
                        b[c] = b[c] - (0.5 * s_in) * (own[c] + at_south)
                        out[c] = out[c] + (pen * s_in) * (at_south - own[c])
                    if g == last:
                        b[c] = b[c] + (0.5 * n_in) * (own[c] + at_north)
                        out[c] = out[c] + (pen * n_in) * (at_north - own[c])
                h = state[s, 0, i, rows(g)]
                u, v = vel_x[s, i, rows(g)], vel_y[s, i, rows(g)]
                cross = a[2] + b[1]
                au, bv = a[1] * u, b[2] * v
                cot = (
                    out[0] + (a[1] + b[2]) * h - au * u - bv * v - cross * (u * v),
                    out[1] + a[0] + 2.0 * au + cross * v,
                    out[2] + b[0] + 2.0 * bv + cross * u,
                )
                for c in comps:
                    adj_ref[c, i, rows(g)] += cot[c]
                    if s > 0:
                        later[c, i, rows(g)] = cot[c]
            if s > 0:
                put_cot(s - 1, i)
            return _

        lax.fori_loop(0, NP, finish_back, 0)

    whole = zs[1]
    for k, peer in line_peers:
        line_copy(k, peer).wait_recv()
        whole = whole + zr[plane + k]
    nodes = events * n_ev * ext_x * n_tx * ext_y * n_ty * NP * NP
    grad_ref[...] = whole[:, :ZONES] * (ZONES / (TIME_STEP * nodes))

    for rnd in range(2 * SECTIONS):
        for side in (EAST, WEST, NORTH, SOUTH):
            @pl.when(has[side])
            def _():
                copy(rnd, side).wait_send()
    for k, peer in plane_peers:
        plane_copy(k, peer).wait_send()
    for k, peer in line_peers:
        line_copy(k, peer).wait_send()


def local(axes, depth0, momentum0, obs_weight, wet_mask, zone_id, manning):
    ext_x, ext_y = depth0.shape[3:]
    rows = NP * ext_x
    field = (NP, rows, ext_y)
    rounds = 2 * SECTIONS
    slots = axes["ty"] * axes["ev"] + axes["tx"]
    f32 = jnp.float32
    vmem = pl.BlockSpec(memory_space=pltpu.VMEM)
    adjoint, grad = pl.pallas_call(
        functools.partial(kernel, axes, ext_x, depth0.shape[0]),
        out_shape=(
            jax.ShapeDtypeStruct((3,) + field, f32),
            jax.ShapeDtypeStruct((1, ZONES), f32),
        ),
        in_specs=[vmem] * 5 + [pl.BlockSpec(memory_space=pltpu.SMEM)],
        out_specs=(vmem, vmem),
        scratch_shapes=[
            pltpu.VMEM((SECTIONS, 3) + field, f32),
            pltpu.VMEM((SECTIONS,) + field, f32),
            pltpu.VMEM((SECTIONS,) + field, f32),
            pltpu.VMEM((SECTIONS,) + field, f32),
            pltpu.VMEM((SECTIONS,) + field, f32),
            pltpu.VMEM((3,) + field, f32),
            pltpu.VMEM((3,) + field, f32),
            pltpu.VMEM((3,) + field, f32),
            pltpu.VMEM((3,) + field, f32),
            pltpu.VMEM((2,) + field, f32),
            pltpu.VMEM((3,) + field, f32),
            pltpu.VMEM((SECTIONS, SUB, ext_y), f32),
            pltpu.VMEM((SUB, ext_y), f32),
            pltpu.VMEM((2, ext_x, ext_x, SUB // ext_x, SUB, ext_y), f32),
            pltpu.VMEM((SUB, ext_y), f32),
            pltpu.VMEM((rounds, 2, 3, SUB, ext_y), f32),
            pltpu.VMEM((rounds, 2, 3, SUB, ext_y), f32),
            pltpu.VMEM((rounds, 2, 3, NP, SUB, ext_y), f32),
            pltpu.VMEM((rounds, 2, 3, NP, SUB, ext_y), f32),
            pltpu.VMEM((2, 1, ext_y), f32),
            pltpu.VMEM((slots, 1, ext_y), f32),
            pltpu.SemaphoreType.DMA((rounds, 4)),
            pltpu.SemaphoreType.DMA((rounds, 4)),
            pltpu.SemaphoreType.DMA((slots,)),
            pltpu.SemaphoreType.DMA((slots,)),
        ],
        compiler_params=pltpu.CompilerParams(
            collective_id=0, has_side_effects=True, vmem_limit_bytes=32 * 1024 * 1024
        ),
    )(
        depth0.reshape(field),
        momentum0.reshape((2,) + field),
        obs_weight.reshape(field),
        wet_mask.reshape(wet_mask.shape[1:]),
        zone_id,
        manning,
    )
    return adjoint.reshape((1, 3, NP, NP, ext_x, ext_y)), grad.reshape((ZONES,))


def solution(mesh):
    in_specs = (
        P(("basin", "ev"), None, None, "tx", "ty"),
        P(("basin", "ev"), None, None, None, "tx", "ty"),
        P(("basin", "ev"), None, None, "tx", "ty"),
        P(("basin", "ev"), None, "tx", "ty"),
        P(("basin", "tx"), "ty"),
        P("basin"),
    )
    out_specs = (P(("basin", "ev"), None, None, None, "tx", "ty"), P("basin"))
    return jax.shard_map(
        functools.partial(local, dict(mesh.shape)),
        mesh=mesh, in_specs=in_specs, out_specs=out_specs, check_vma=False,
    )
```

profile of v0, /device:TPU:0, one launch (start us, length us, event | category | flops | bytes accessed | tf_op | source)
XLA Modules:
  0.0 42.6 jit_solution(561694038091246518)
XLA Ops:
  0.6 0.0 copy-start.3
  0.6 0.0 copy-start.4
  0.7 0.0 copy-start.5
  0.7 0.7 %copy-done.3 = s32[1,4,2,128]{3,2,1,0:T(2,128)S(1)} copy-done((s32[1,4,2,128]{3,2,1,0:T(2,128)S(1)}, s32[1,4,2,128]{3,2,1,0:T(2,128)}, u32[]{:S(2)}) %copy-start.3) | copy-done | bytes 4120
  1.3 0.0 copy-done.4
  1.3 0.0 copy-done.5
  1.3 0.0 copy-start
  1.3 0.9 %copy-done = f32[1,2,8,8,2,128]{5,4,3,2,1,0:T(2,128)S(1)} copy-done((f32[1,2,8,8,2,128]{5,4,3,2,1,0:T(2,128)S(1)}, f32[1,2,8,8,2,128]{5,4,3,2,1,0:T(2,128)}, u32[]{:S(2)}) %copy-start) | copy-done | bytes 131096
  2.2 0.0 copy-start.1
  2.2 0.8 %copy-done.1 = f32[1,8,8,2,128]{4,3,2,1,0:T(2,128)S(1)} copy-done((f32[1,8,8,2,128]{4,3,2,1,0:T(2,128)S(1)}, f32[1,8,8,2,128]{4,3,2,1,0:T(2,128)}, u32[]{:S(2)}) %copy-start.1) | copy-done | bytes 65560
  3.1 0.0 copy-start.2
  3.1 0.8 %copy-done.2 = f32[1,8,8,2,128]{4,3,2,1,0:T(2,128)S(1)} copy-done((f32[1,8,8,2,128]{4,3,2,1,0:T(2,128)S(1)}, f32[1,8,8,2,128]{4,3,2,1,0:T(2,128)}, u32[]{:S(2)}) %copy-start.2) | copy-done | bytes 65560
  3.9 37.5 %shard_map.77 = (f32[3,8,16,128]{3,2,1,0:T(8,128)S(1)}, f32[1,32]{1,0:T(1,128)S(1)}) custom-call(f32[8,16,128]{2,1,0:T(8,128)S(1)} %bitcast.8, f32[2,8,16,128]{3,2,1,0:T(8,128)S(1)} %bitcast.7, f32[8,16,128]{2,1,0:T(8,128)S(1)} %bitcast.9, s32[4,2,128]{2,1,0:T(2,128)S(1)} %bitcast.10, s32[2,128]{1,0:T(2,128)S(1)} %copy-done.4, f32[32]{0:T(128)S(1)} %copy-done.5), custom_call_target="tpu_custom_call" | custom-call | tf_op jit(solution)/shard_map/pallas_call | solution.py:495
  41.4 0.7 %copy.10 = f32[1,3,8,8,2,128]{5,4,3,2,1,0:T(2,128)} copy(f32[1,3,8,8,2,128]{5,4,3,2,1,0:T(2,128)S(1)} %bitcast.6) | data formatting | bytes 393216
  42.1 0.5 %copy.11 = f32[32]{0:T(128)} copy(f32[32]{0:T(128)S(1)} %bitcast.11) | data formatting | bytes 256
Async XLA Ops:
  0.6 0.7 %copy-start.3 = (s32[1,4,2,128]{3,2,1,0:T(2,128)S(1)}, s32[1,4,2,128]{3,2,1,0:T(2,128)}, u32[]{:S(2)}) copy-start(s32[1,4,2,128]{3,2,1,0:T(2,128)} %param.9) | copy-start | bytes 12292
  0.6 0.7 %copy-start.4 = (s32[2,128]{1,0:T(2,128)S(1)}, s32[2,128]{1,0:T(2,128)}, u32[]{:S(2)}) copy-start(s32[2,128]{1,0:T(2,128)} %zone_ref.1) | copy-start | bytes 3076
  0.7 0.7 %copy-start.5 = (f32[32]{0:T(128)S(1)}, f32[32]{0:T(128)}, u32[]{:S(2)}) copy-start(f32[32]{0:T(128)} %manning_ref.1) | copy-start | bytes 388
  1.3 0.9 %copy-start = (f32[1,2,8,8,2,128]{5,4,3,2,1,0:T(2,128)S(1)}, f32[1,2,8,8,2,128]{5,4,3,2,1,0:T(2,128)}, u32[]{:S(2)}) copy-start(f32[1,2,8,8,2,128]{5,4,3,2,1,0:T(2,128)} %param.7) | copy-start | bytes 393220
  2.2 0.8 %copy-start.1 = (f32[1,8,8,2,128]{4,3,2,1,0:T(2,128)S(1)}, f32[1,8,8,2,128]{4,3,2,1,0:T(2,128)}, u32[]{:S(2)}) copy-start(f32[1,8,8,2,128]{4,3,2,1,0:T(2,128)} %param.6) | copy-start | bytes 196612
  3.1 0.8 %copy-start.2 = (f32[1,8,8,2,128]{4,3,2,1,0:T(2,128)S(1)}, f32[1,8,8,2,128]{4,3,2,1,0:T(2,128)}, u32[]{:S(2)}) copy-start(f32[1,8,8,2,128]{4,3,2,1,0:T(2,128)} %param.8) | copy-start | bytes 196612
where the time goes:
time: 42.9 us; the launch traced here: 42.6 us
  Pallas kernels  37.5 us (87%)
  local copies, waits for them, and re-layouts  4.45 us (10%)
  between operations  0.67 us (2%)
    pallas_call x1, Pallas kernels, local(): pl.pallas_call(functools.partial(kernel, axes, ext_x, depth0.shape[0]), o...  37.5 us
    unnamed x14, local copies, waits for them, and re-layouts  4.45 us

commit v1 on v0

v1 whole, which is shorter than its diff:
```python
import functools

import jax
import jax.numpy as jnp
import numpy as np
from jax import lax
from jax.experimental import pallas as pl
from jax.experimental.pallas import tpu as pltpu
from jax.sharding import PartitionSpec as P

NP = 8
SECTIONS = 4
ZONES = 32
SUB = 8

PENALTY_SPEED = 4.0
TIME_STEP = 0.0005
SPEED_FLOOR = 0.01
MESH = pl.DeviceIdType.MESH
EAST, WEST, NORTH, SOUTH = range(4)


def node_tables():
    points = -np.cos(np.pi * np.arange(NP) / (NP - 1))
    identity = np.eye(NP)
    differ = points[:, None] - points[None, :] + identity
    barycentric = 1.0 / np.prod(differ, axis=1)
    derivative = barycentric[None, :] / barycentric[:, None] / differ * (1.0 - identity)
    derivative = derivative - identity * derivative.sum(axis=1)[:, None]
    order = NP - 1
    end_weight = 1.0 / (order * order)
    return (derivative, float(1.0 / end_weight))


def along_first(table, slabs):
    half = NP // 2
    even = [slabs[k] + slabs[NP - 1 - k] for k in range(half)]
    odd = [slabs[k] - slabs[NP - 1 - k] for k in range(half)]
    out = [None] * NP
    for a in range(half):
        on_even = sum(float(0.5 * (table[a, k] + table[a, NP - 1 - k])) * even[k] for k in range(half))
        on_odd = sum(float(0.5 * (table[a, k] - table[a, NP - 1 - k])) * odd[k] for k in range(half))
        out[a] = on_odd + on_even
        out[NP - 1 - a] = on_odd - on_even
    return out


def kernel(
    axes, ext_x, events,
    depth_hbm, mom_hbm, weight_hbm, wet_hbm, zone_hbm, manning_hbm,
    adj_ref, grad_ref,
    mom_ref, weight_ref, wet_ref, zone_ref, manning_ref, in_sem,
    state, vel_x, vel_y, inv_h, drag_r, flux_x, flux_y, tend, acc, final_adj, later,
    wet_rows, rough_rows, coef_y, zone_acc,
    xs, xr, ys, yr, zs, zr, send_sem, recv_sem, zsend_sem, zrecv_sem,
):
    table, lift = node_tables()
    n_tx, n_ty, n_ev = axes["tx"], axes["ty"], axes["ev"]
    tx, ty, ev = lax.axis_index("tx"), lax.axis_index("ty"), lax.axis_index("ev")
    ext_y = depth_hbm.shape[-1]
    groups = ext_x
    step = ext_x
    per = SUB // ext_x
    blocks = NP // per
    has = {EAST: tx < n_tx - 1, WEST: tx > 0, NORTH: ty < n_ty - 1, SOUTH: ty > 0}
    target = {EAST: {"tx": tx + 1}, WEST: {"tx": tx - 1}, NORTH: {"ty": ty + 1}, SOUTH: {"ty": ty - 1}}
    opposite = {EAST: WEST, WEST: EAST, NORTH: SOUTH, SOUTH: NORTH}

    arrive = [
        pltpu.make_async_copy(source, target_ref, in_sem.at[n])
        for n, (source, target_ref) in enumerate((
            (zone_hbm, zone_ref), (manning_hbm, manning_ref), (wet_hbm, wet_ref),
            (depth_hbm, state.at[0, 0]), (mom_hbm, mom_ref), (weight_hbm, weight_ref),
        ))
    ]
    for piece in arrive:
        piece.start()

    plane = n_ty * n_ev
    here = ty * n_ev + ev
    barrier = pltpu.get_barrier_semaphore()
    plane_peers = []
    for k in range(1, plane):
        other = lax.rem(here + k, plane)
        plane_peers.append((k, {"ty": other // n_ev, "ev": lax.rem(other, n_ev)}))
    line_peers = [(k, {"tx": lax.rem(tx + k, n_tx)}) for k in range(1, n_tx)]
    for _, peer in plane_peers + line_peers:
        pl.semaphore_signal(barrier, inc=1, device_id=peer, device_id_type=MESH)

    sub = lax.broadcasted_iota(jnp.int32, (SUB, ext_y), 0)
    lane = lax.broadcasted_iota(jnp.int32, (SUB, ext_y), 1)
    elem = lax.rem(sub, ext_x)

    def flag(yes):
        return jnp.where(yes, 1, 0)

    zero = jnp.float32(0.0)
    inside = {
        WEST: jnp.where((elem == 0) & (flag(has[WEST]) == 0), zero, lift),
        EAST: jnp.where((elem == ext_x - 1) & (flag(has[EAST]) == 0), zero, lift),
        SOUTH: jnp.where((sub >= ext_x) | ((lane == 0) & (flag(has[SOUTH]) == 0)), zero, lift),
        NORTH: jnp.where((sub < SUB - ext_x) | ((lane == ext_y - 1) & (flag(has[NORTH]) == 0)), zero, lift),
    }
    first_elem = (elem == 0) & (flag(has[WEST]) == 1)
    last_elem = (elem == ext_x - 1) & (flag(has[EAST]) == 1)
    first_lane = (lane == 0) & (flag(has[SOUTH]) == 1)
    last_lane = (lane == ext_y - 1) & (flag(has[NORTH]) == 1)

    def spread(rows):
        out = jnp.broadcast_to(rows[0:1], (SUB, ext_y))
        for e in range(1, ext_x):
            out = jnp.where(elem == e, jnp.broadcast_to(rows[e:e + 1], (SUB, ext_y)), out)
        return out

    for t, mat in enumerate((table, table.T)):
        for g in range(groups):
            for h in range(groups):
                for k in range(SUB // step):
                    column = jnp.zeros((SUB, ext_y), jnp.float32)
                    for r in range(SUB):
                        a = (SUB * g + r) // ext_x
                        b = (SUB * h + (r - k * step) % SUB) // ext_x
                        column = jnp.where(sub == r, jnp.float32(-mat[a, b]), column)
                    coef_y[t, g, h, k] = column
    for piece in arrive[:3]:
        piece.wait()
    for s in range(SECTIONS):
        wet_rows[s] = spread(wet_ref[s].astype(jnp.float32))
    zone = spread(zone_ref[...])
    rough = jnp.zeros((SUB, ext_y), jnp.float32)
    for z in range(ZONES):
        rough = jnp.where(zone == z, manning_ref[z], rough)
    rough_rows[...] = rough

    zone_acc[...] = jnp.zeros((SUB, ext_y), jnp.float32)

    def rows(g):
        return pl.ds(SUB * g, SUB)

    def roll(value, shift, axis):
        size = value.shape[axis]
        shift = shift % size
        return value if shift == 0 else pltpu.roll(value, shift, axis)

    def load_coef(t):
        return [[[coef_y[t, g, h, k] for k in range(per)] for h in range(groups)] for g in range(groups)]

    def minus_along_second(coef, source):
        turned = [[roll(source[h], k * step, 0) for k in range(per)] for h in range(groups)]
        return [
            sum(coef[g][h][k] * turned[h][k] for h in range(groups) for k in range(per))
            for g in range(groups)
        ]

    def copy(rnd, side):
        pair, slot = ((xs, xr), side) if side in (EAST, WEST) else ((ys, yr), side - 2)
        return pltpu.make_async_remote_copy(
            src_ref=pair[0].at[rnd, slot],
            dst_ref=pair[1].at[rnd, slot],
            send_sem=send_sem.at[rnd, side],
            recv_sem=recv_sem.at[rnd, side],
            device_id=target[side],
            device_id_type=MESH,
        )

    def start(rnd, sides):
        for side in sides:
            @pl.when(has[side])
            def _():
                copy(rnd, side).start()

    def await_all(rnd, sides):
        for side in sides:
            @pl.when(has[opposite[side]])
            def _():
                copy(rnd, side).wait_recv()

    def pack_x(rnd, c, east, west):
        to_east, to_west = east[0], west[0]
        for g in range(1, groups):
            to_east = jnp.where(elem == ext_x - 1 - g, roll(east[g], -g, 0), to_east)
            to_west = jnp.where(elem == g, roll(west[g], g, 0), to_west)
        xs[rnd, EAST, c] = to_east
        xs[rnd, WEST, c] = to_west

    def beside_x(rnd, c, g, east, west):
        from_west, from_east = xr[rnd, EAST, c], xr[rnd, WEST, c]
        at_west = jnp.where(first_elem, roll(from_west, -(ext_x - 1 - g), 0), roll(east[g], 1, 0))
        at_east = jnp.where(last_elem, roll(from_east, ext_x - 1 - g, 0), roll(west[g], -1, 0))
        return at_west, at_east

    slot_of = sub // ext_x

    def pack_y(rnd, c, blk, north, south):
        to_north, to_south = roll(north[0], ext_x, 0), south[0]
        for k in range(1, per):
            to_north = jnp.where(slot_of == k, roll(north[k], (k + 1) * ext_x, 0), to_north)
            to_south = jnp.where(slot_of == k, roll(south[k], k * ext_x, 0), to_south)
        ys[rnd, 0, c, blk] = roll(to_north, 1, 1)
        ys[rnd, 1, c, blk] = roll(to_south, -1, 1)

    def beside_y(rnd, c, blk):
        at_south = jnp.where(first_lane, yr[rnd, 0, c, blk], ys[rnd, 0, c, blk])
        at_north = jnp.where(last_lane, yr[rnd, 1, c, blk], ys[rnd, 1, c, blk])
        return (
            [roll(at_south, -k * ext_x, 0) for k in range(per)],
            [roll(at_north, -(k + 1) * ext_x, 0) for k in range(per)],
        )

    first, last = 0, groups - 1
    comps = range(3)
    pen = 0.5 * PENALTY_SPEED

    def put_fluxes(s, blk):
        north, south = [[] for c in comps], [[] for c in comps]
        for n in range(per):
            i = blk * per + n
            for g in range(groups):
                h, p, m = (state[s, c, i, rows(g)] for c in comps)
                ih = 1.0 / h
                u, v = p * ih, m * ih
                inv_h[s, i, rows(g)] = ih
                vel_x[s, i, rows(g)] = u
                vel_y[s, i, rows(g)] = v
                pressure = 0.5 * h * h
                cross = p * v
                fx = (p, p * u + pressure, cross)
                fy = (m, cross, m * v + pressure)
                for c, q in enumerate((h, p, m)):
                    flux_x[c, i, rows(g)] = fx[c]
                    flux_y[c, i, rows(g)] = fy[c]
                    if g == last:
                        north[c].append(0.5 * fy[c] + pen * q)
                    if g == first:
                        south[c].append(pen * q - 0.5 * fy[c])
        for c in comps:
            pack_y(s, c, blk, north[c], south[c])

    def x_traces(s, c):
        east = [0.5 * flux_x[c, NP - 1, rows(g)] + pen * state[s, c, NP - 1, rows(g)] for g in range(groups)]
        west = [pen * state[s, c, 0, rows(g)] - 0.5 * flux_x[c, 0, rows(g)] for g in range(groups)]
        return east, west

    coefs = (0.5 * TIME_STEP, 0.5 * TIME_STEP, TIME_STEP)
    sums = (1.0, 2.0, 2.0, 1.0)
    final_weights = (TIME_STEP / 6.0, TIME_STEP / 3.0, TIME_STEP / 3.0, TIME_STEP / 6.0)

    def send_forward(s):
        for c in comps:
            pack_x(s, c, *x_traces(s, c))
        start(s, (EAST, WEST, NORTH, SOUTH))

    def set_up(i, _):
        for k in range(per):
            state[0, 1, i * per + k] = mom_ref[0, i * per + k]
            state[0, 2, i * per + k] = mom_ref[1, i * per + k]
        put_fluxes(0, i)
        return _

    for piece in arrive[3:]:
        piece.wait()
    lax.fori_loop(0, blocks, set_up, 0)
    pl.semaphore_wait(barrier, len(plane_peers) + len(line_peers))
    send_forward(0)

    for s in range(SECTIONS):
        def volume(blk, _):
            coef = load_coef(0)
            rough_g = rough_rows[...]
            for n in range(per):
                i = blk * per + n
                out = [minus_along_second(coef, [flux_y[c, i, rows(g)] for g in range(groups)]) for c in comps]
                for g in range(groups):
                    h, p, m = (state[s, c, i, rows(g)] for c in comps)
                    u, v = vel_x[s, i, rows(g)], vel_y[s, i, rows(g)]
                    speed = jnp.sqrt(u * u + v * v + SPEED_FLOOR)
                    kr = rough_g * speed * jnp.exp((-4.0 / 3.0) * jnp.log(h))
                    drag_r[s, i, rows(g)] = kr
                    k = rough_g * kr
                    tend[0, i, rows(g)] = out[0][g]
                    tend[1, i, rows(g)] = out[1][g] - k * p
                    tend[2, i, rows(g)] = out[2][g] - k * m
            return _

        lax.fori_loop(0, blocks, volume, 0)

        def volume_x(c, _):
            for g in range(groups):
                out = along_first(table, [flux_x[c, i, rows(g)] for i in range(NP)])
                for i in range(NP):
                    tend[c, i, rows(g)] -= out[i]
            return _

        lax.fori_loop(0, 3, volume_x, 0)

        await_all(s, (EAST, WEST, NORTH, SOUTH))
        for c in comps:
            east, west = x_traces(s, c)
            for g in range(groups):
                at_west, at_east = beside_x(s, c, g, east, west)
                q0, q7 = state[s, c, 0, rows(g)], state[s, c, NP - 1, rows(g)]
                f0, f7 = flux_x[c, 0, rows(g)], flux_x[c, NP - 1, rows(g)]
                tend[c, 0, rows(g)] += (inside[WEST]) * (at_west - (0.5 * f0 + pen * q0))
                tend[c, NP - 1, rows(g)] += (inside[EAST]) * (at_east - (pen * q7 - 0.5 * f7))

        def finish(blk, _):
            wet = wet_rows[s]
            for c in comps:
                at_south, at_north = beside_y(s, c, blk)
                for n in range(per):
                    i = blk * per + n
                    for g in range(groups):
                        slope = tend[c, i, rows(g)]
                        if g == first:
                            own = 0.5 * flux_y[c, i, rows(g)] + pen * state[s, c, i, rows(g)]
                            slope = slope + inside[SOUTH] * (at_south[n] - own)
                        if g == last:
                            own = pen * state[s, c, i, rows(g)] - 0.5 * flux_y[c, i, rows(g)]
                            slope = slope + inside[NORTH] * (at_north[n] - own)
                        slope = wet * slope
                        start_q = state[0, c, i, rows(g)]
                        if s == 0:
                            acc[c, i, rows(g)] = slope
                        elif s < SECTIONS - 1:
                            acc[c, i, rows(g)] += sums[s] * slope
                        if s < SECTIONS - 1:
                            state[s + 1, c, i, rows(g)] = start_q + coefs[s] * slope
                        elif c > 0:
                            total = acc[c, i, rows(g)] + slope
                            final = start_q + (TIME_STEP / 6.0) * total
                            seed = weight_ref[i, rows(g)] * final
                            final_adj[c - 1, i, rows(g)] = seed
                            adj_ref[c, i, rows(g)] = seed
                        else:
                            adj_ref[c, i, rows(g)] = jnp.zeros((SUB, ext_y), jnp.float32)
            if s < SECTIONS - 1:
                put_fluxes(s + 1, blk)
            else:
                put_cot(s, blk)
            return _

        def put_cot(s, blk):
            wet = wet_rows[s]
            for c in comps:
                north, south = [], []
                for n in range(per):
                    i = blk * per + n
                    for g in range(groups):
                        value = None
                        if c > 0:
                            value = final_weights[s] * final_adj[c - 1, i, rows(g)]
                        if s < SECTIONS - 1:
                            back = coefs[s] * later[c, i, rows(g)]
                            value = back if value is None else value + back
                        if value is None:
                            value = jnp.zeros((SUB, ext_y), jnp.float32)
                        value = wet * value
                        acc[c, i, rows(g)] = value
                        if g == last:
                            north.append(value)
                        if g == first:
                            south.append(value)
                pack_y(2 * SECTIONS - 1 - s, c, blk, north, south)

        lax.fori_loop(0, blocks, finish, 0)
        if s < SECTIONS - 1:
            send_forward(s + 1)

    def cot_faces(c):
        return (
            [acc[c, NP - 1, rows(g)] for g in range(groups)],
            [acc[c, 0, rows(g)] for g in range(groups)],
        )

    def plane_copy(k, peer):
        return pltpu.make_async_remote_copy(
            src_ref=zs.at[0], dst_ref=zr.at[k],
            send_sem=zsend_sem.at[k], recv_sem=zrecv_sem.at[k],
            device_id=peer, device_id_type=MESH,
        )

    def line_copy(k, peer):
        slot = plane + k
        return pltpu.make_async_remote_copy(
            src_ref=zs.at[1], dst_ref=zr.at[slot],
            send_sem=zsend_sem.at[slot], recv_sem=zrecv_sem.at[slot],
            device_id=peer, device_id_type=MESH,
        )

    for s in reversed(range(SECTIONS)):
        rnd = 2 * SECTIONS - 1 - s
        for c in comps:
            pack_x(rnd, c, *cot_faces(c))
        start(rnd, (EAST, WEST, NORTH, SOUTH))

        def drag_back(blk, _):
            rough_g = rough_rows[...]
            parts = []
            for n in range(per):
                i = blk * per + n
                for g in range(groups):
                    h, p, m = (state[s, c, i, rows(g)] for c in comps)
                    u, v, ih = vel_x[s, i, rows(g)], vel_y[s, i, rows(g)], inv_h[s, i, rows(g)]
                    kr = drag_r[s, i, rows(g)]
                    c1, c2 = acc[1, i, rows(g)], acc[2, i, rows(g)]
                    part = kr * (c1 * p + c2 * m)
                    parts.append(part)
                    k = rough_g * kr
                    e = rough_g * part * ih
                    square = u * u + v * v
                    eq = e / (square + SPEED_FLOOR)
                    tend[0, i, rows(g)] = (4.0 / 3.0) * e + eq * square
                    tend[1, i, rows(g)] = -(k * c1 + eq * u)
                    tend[2, i, rows(g)] = -(k * c2 + eq * v)
            zone_acc[...] += sum(parts)
            return _

        lax.fori_loop(0, blocks, drag_back, 0)

        if s == 0:
            total = zone_acc[...]
            shift = ext_x
            while shift < SUB:
                total = total + roll(total, shift, 0)
                shift *= 2
            total = -2.0 * total
            zones = lax.broadcasted_iota(jnp.int32, (ZONES, ext_y), 0)
            spot = jnp.zeros((ZONES, ext_y), jnp.float32)
            for e in range(ext_x):
                ids = jnp.broadcast_to(zone_ref[e:e + 1, :], (ZONES, ext_y))
                spot = spot + jnp.where(ids == zones, jnp.broadcast_to(total[e:e + 1], (ZONES, ext_y)), 0.0)
            per_zone = jnp.sum(spot, axis=1, keepdims=True)
            spots = lax.broadcasted_iota(jnp.int32, (ZONES, ext_y), 1)
            line = jnp.sum(jnp.where(zones == spots, jnp.broadcast_to(per_zone, (ZONES, ext_y)), 0.0), axis=0, keepdims=True)
            zs[0] = line
            for k, peer in plane_peers:
                plane_copy(k, peer).start()

        def volume_y(blk, _):
            coef = load_coef(1)
            for n in range(per):
                i = blk * per + n
                for c in comps:
                    out = minus_along_second(coef, [acc[c, i, rows(g)] for g in range(groups)])
                    for g in range(groups):
                        flux_y[c, i, rows(g)] = out[g]
            return _

        lax.fori_loop(0, blocks, volume_y, 0)

        def volume_back(c, _):
            for g in range(groups):
                out = along_first(-table.T, [acc[c, i, rows(g)] for i in range(NP)])
                for i in range(NP):
                    flux_x[c, i, rows(g)] = out[i]
            return _

        lax.fori_loop(0, 3, volume_back, 0)

        await_all(rnd, (EAST, WEST, NORTH, SOUTH))
        if s == 0:
            mine = zs[0]
            for k, peer in plane_peers:
                plane_copy(k, peer).wait_recv()
                mine = mine + zr[k]
            zs[1] = mine
            for k, peer in line_peers:
                line_copy(k, peer).start()
        for c in comps:
            east, west = cot_faces(c)
            for g in range(groups):
                at_west, at_east = beside_x(rnd, c, g, east, west)
                w_in, e_in = inside[WEST], inside[EAST]
                flux_x[c, 0, rows(g)] -= (0.5 * w_in) * (west[g] + at_west)
                tend[c, 0, rows(g)] += (pen * w_in) * (at_west - west[g])
                flux_x[c, NP - 1, rows(g)] += (0.5 * e_in) * (east[g] + at_east)
                tend[c, NP - 1, rows(g)] += (pen * e_in) * (at_east - east[g])

        def finish_back(blk, _):
            s_in, n_in = inside[SOUTH], inside[NORTH]
            beside = [beside_y(rnd, c, blk) for c in comps]
            for n in range(per):
                i = blk * per + n
                for g in range(groups):
                    a = [flux_x[c, i, rows(g)] for c in comps]
                    b = [flux_y[c, i, rows(g)] for c in comps]
                    out = [tend[c, i, rows(g)] for c in comps]
                    own = [acc[c, i, rows(g)] for c in comps]
                    for c in comps:
                        if g == first:
                            there = beside[c][0][n]
                            b[c] = b[c] - (0.5 * s_in) * (own[c] + there)
                            out[c] = out[c] + (pen * s_in) * (there - own[c])
                        if g == last:
                            there = beside[c][1][n]
                            b[c] = b[c] + (0.5 * n_in) * (own[c] + there)
                            out[c] = out[c] + (pen * n_in) * (there - own[c])
                    h = state[s, 0, i, rows(g)]
                    u, v = vel_x[s, i, rows(g)], vel_y[s, i, rows(g)]
                    cross = a[2] + b[1]
                    au, bv = a[1] * u, b[2] * v
                    cot = (
                        out[0] + (a[1] + b[2]) * h - au * u - bv * v - cross * (u * v),
                        out[1] + a[0] + 2.0 * au + cross * v,
                        out[2] + b[0] + 2.0 * bv + cross * u,
                    )
                    for c in comps:
                        adj_ref[c, i, rows(g)] += cot[c]
                        if s > 0:
                            later[c, i, rows(g)] = cot[c]
            if s > 0:
                put_cot(s - 1, blk)
            return _

        lax.fori_loop(0, blocks, finish_back, 0)

    whole = zs[1]
    for k, peer in line_peers:
        line_copy(k, peer).wait_recv()
        whole = whole + zr[plane + k]
    nodes = events * n_ev * ext_x * n_tx * ext_y * n_ty * NP * NP
    grad_ref[...] = whole[:, :ZONES] * (ZONES / (TIME_STEP * nodes))

    for rnd in range(2 * SECTIONS):
        for side in (EAST, WEST, NORTH, SOUTH):
            @pl.when(has[side])
            def _():
                copy(rnd, side).wait_send()
    for k, peer in plane_peers:
        plane_copy(k, peer).wait_send()
    for k, peer in line_peers:
        line_copy(k, peer).wait_send()


def local(axes, depth0, momentum0, obs_weight, wet_mask, zone_id, manning):
    ext_x, ext_y = depth0.shape[3:]
    rows = NP * ext_x
    field = (NP, rows, ext_y)
    rounds = 2 * SECTIONS
    slots = axes["ty"] * axes["ev"] + axes["tx"]
    f32 = jnp.float32
    vmem = pl.BlockSpec(memory_space=pltpu.VMEM)
    adjoint, grad = pl.pallas_call(
        functools.partial(kernel, axes, ext_x, depth0.shape[0]),
        out_shape=(
            jax.ShapeDtypeStruct((3,) + field, f32),
            jax.ShapeDtypeStruct((1, ZONES), f32),
        ),
        in_specs=[pl.BlockSpec(memory_space=pltpu.HBM)] * 6,
        out_specs=(vmem, vmem),
        scratch_shapes=[
            pltpu.VMEM((2,) + field, f32),
            pltpu.VMEM(field, f32),
            pltpu.VMEM(wet_mask.shape[1:], jnp.int32),
            pltpu.VMEM(zone_id.shape, jnp.int32),
            pltpu.SMEM(manning.shape, f32),
            pltpu.SemaphoreType.DMA((6,)),
            pltpu.VMEM((SECTIONS, 3) + field, f32),
            pltpu.VMEM((SECTIONS,) + field, f32),
            pltpu.VMEM((SECTIONS,) + field, f32),
            pltpu.VMEM((SECTIONS,) + field, f32),
            pltpu.VMEM((SECTIONS,) + field, f32),
            pltpu.VMEM((3,) + field, f32),
            pltpu.VMEM((3,) + field, f32),
            pltpu.VMEM((3,) + field, f32),
            pltpu.VMEM((3,) + field, f32),
            pltpu.VMEM((2,) + field, f32),
            pltpu.VMEM((3,) + field, f32),
            pltpu.VMEM((SECTIONS, SUB, ext_y), f32),
            pltpu.VMEM((SUB, ext_y), f32),
            pltpu.VMEM((2, ext_x, ext_x, SUB // ext_x, SUB, ext_y), f32),
            pltpu.VMEM((SUB, ext_y), f32),
            pltpu.VMEM((rounds, 2, 3, SUB, ext_y), f32),
            pltpu.VMEM((rounds, 2, 3, SUB, ext_y), f32),
            pltpu.VMEM((rounds, 2, 3, NP // (SUB // ext_x), SUB, ext_y), f32),
            pltpu.VMEM((rounds, 2, 3, NP // (SUB // ext_x), SUB, ext_y), f32),
            pltpu.VMEM((2, 1, ext_y), f32),
            pltpu.VMEM((slots, 1, ext_y), f32),
            pltpu.SemaphoreType.DMA((rounds, 4)),
            pltpu.SemaphoreType.DMA((rounds, 4)),
            pltpu.SemaphoreType.DMA((slots,)),
            pltpu.SemaphoreType.DMA((slots,)),
        ],
        compiler_params=pltpu.CompilerParams(
            collective_id=0, has_side_effects=True, vmem_limit_bytes=32 * 1024 * 1024
        ),
    )(
        depth0.reshape(field),
        momentum0.reshape((2,) + field),
        obs_weight.reshape(field),
        wet_mask.reshape(wet_mask.shape[1:]),
        zone_id,
        manning,
    )
    return adjoint.reshape((1, 3, NP, NP, ext_x, ext_y)), grad.reshape((ZONES,))


def solution(mesh):
    in_specs = (
        P(("basin", "ev"), None, None, "tx", "ty"),
        P(("basin", "ev"), None, None, None, "tx", "ty"),
        P(("basin", "ev"), None, None, "tx", "ty"),
        P(("basin", "ev"), None, "tx", "ty"),
        P(("basin", "tx"), "ty"),
        P("basin"),
    )
    out_specs = (P(("basin", "ev"), None, None, None, "tx", "ty"), P("basin"))
    return jax.shard_map(
        functools.partial(local, dict(mesh.shape)),
        mesh=mesh, in_specs=in_specs, out_specs=out_specs, check_vma=False,
    )
```

time: 42.9 us -> 39.1 us (0.911)
  Pallas kernels: 37.5 us -> 33.7 us
    pallas_call x1, Pallas kernels: 37.5 us -> 33.7 us  [local(): pl.pallas_call(functools.partial(kernel, axes, ext_x, depth0.shape[0]), o...]
where the time goes in v1:
time: 39.1 us; the launch traced here: 38.8 us
  Pallas kernels  33.7 us (86%)
  local copies, waits for them, and re-layouts  4.45 us (11%)
  between operations  0.67 us (2%)
    pallas_call x1, Pallas kernels, local(): pl.pallas_call(functools.partial(kernel, axes, ext_x, depth0.shape[0]), o...  33.7 us
    unnamed x14, local copies, waits for them, and re-layouts  4.45 us

profile of v1, /device:TPU:0, one launch (start us, length us, event | category | flops | bytes accessed | tf_op | source)
XLA Modules:
  0.0 38.8 jit_solution(3690937602799300633)
XLA Ops:
  0.6 0.0 copy-start.3
  0.6 0.0 copy-start.4
  0.7 0.0 copy-start.5
  0.7 0.7 %copy-done.3 = s32[1,4,2,128]{3,2,1,0:T(2,128)S(1)} copy-done((s32[1,4,2,128]{3,2,1,0:T(2,128)S(1)}, s32[1,4,2,128]{3,2,1,0:T(2,128)}, u32[]{:S(2)}) %copy-start.3) | copy-done | bytes 4120
  1.3 0.0 copy-done.4
  1.3 0.0 copy-done.5
  1.3 0.0 copy-start
  1.3 0.9 %copy-done = f32[1,2,8,8,2,128]{5,4,3,2,1,0:T(2,128)S(1)} copy-done((f32[1,2,8,8,2,128]{5,4,3,2,1,0:T(2,128)S(1)}, f32[1,2,8,8,2,128]{5,4,3,2,1,0:T(2,128)}, u32[]{:S(2)}) %copy-start) | copy-done | bytes 131096
  2.2 0.0 copy-start.1
  2.2 0.8 %copy-done.1 = f32[1,8,8,2,128]{4,3,2,1,0:T(2,128)S(1)} copy-done((f32[1,8,8,2,128]{4,3,2,1,0:T(2,128)S(1)}, f32[1,8,8,2,128]{4,3,2,1,0:T(2,128)}, u32[]{:S(2)}) %copy-start.1) | copy-done | bytes 65560
  3.1 0.0 copy-start.2
  3.1 0.8 %copy-done.2 = f32[1,8,8,2,128]{4,3,2,1,0:T(2,128)S(1)} copy-done((f32[1,8,8,2,128]{4,3,2,1,0:T(2,128)S(1)}, f32[1,8,8,2,128]{4,3,2,1,0:T(2,128)}, u32[]{:S(2)}) %copy-start.2) | copy-done | bytes 65560
  3.9 33.7 %shard_map.77 = (f32[3,8,16,128]{3,2,1,0:T(8,128)S(1)}, f32[1,32]{1,0:T(1,128)S(1)}) custom-call(f32[8,16,128]{2,1,0:T(8,128)S(1)} %bitcast.8, f32[2,8,16,128]{3,2,1,0:T(8,128)S(1)} %bitcast.7, f32[8,16,128]{2,1,0:T(8,128)S(1)} %bitcast.9, s32[4,2,128]{2,1,0:T(2,128)S(1)} %bitcast.10, s32[2,128]{1,0:T(2,128)S(1)} %copy-done.4, f32[32]{0:T(128)S(1)} %copy-done.5), custom_call_target="tpu_custom_call" | custom-call | tf_op jit(solution)/shard_map/pallas_call | solution.py:543
  37.6 0.7 %copy.10 = f32[1,3,8,8,2,128]{5,4,3,2,1,0:T(2,128)} copy(f32[1,3,8,8,2,128]{5,4,3,2,1,0:T(2,128)S(1)} %bitcast.6) | data formatting | bytes 393216
  38.3 0.5 %copy.11 = f32[32]{0:T(128)} copy(f32[32]{0:T(128)S(1)} %bitcast.11) | data formatting | bytes 256
Async XLA Ops:
  0.6 0.7 %copy-start.3 = (s32[1,4,2,128]{3,2,1,0:T(2,128)S(1)}, s32[1,4,2,128]{3,2,1,0:T(2,128)}, u32[]{:S(2)}) copy-start(s32[1,4,2,128]{3,2,1,0:T(2,128)} %param.9) | copy-start | bytes 12292
  0.6 0.7 %copy-start.4 = (s32[2,128]{1,0:T(2,128)S(1)}, s32[2,128]{1,0:T(2,128)}, u32[]{:S(2)}) copy-start(s32[2,128]{1,0:T(2,128)} %zone_hbm.1) | copy-start | bytes 3076
  0.7 0.7 %copy-start.5 = (f32[32]{0:T(128)S(1)}, f32[32]{0:T(128)}, u32[]{:S(2)}) copy-start(f32[32]{0:T(128)} %manning_hbm.1) | copy-start | bytes 388
  1.3 0.9 %copy-start = (f32[1,2,8,8,2,128]{5,4,3,2,1,0:T(2,128)S(1)}, f32[1,2,8,8,2,128]{5,4,3,2,1,0:T(2,128)}, u32[]{:S(2)}) copy-start(f32[1,2,8,8,2,128]{5,4,3,2,1,0:T(2,128)} %param.7) | copy-start | bytes 393220
  2.2 0.8 %copy-start.1 = (f32[1,8,8,2,128]{4,3,2,1,0:T(2,128)S(1)}, f32[1,8,8,2,128]{4,3,2,1,0:T(2,128)}, u32[]{:S(2)}) copy-start(f32[1,8,8,2,128]{4,3,2,1,0:T(2,128)} %param.6) | copy-start | bytes 196612
  3.1 0.8 %copy-start.2 = (f32[1,8,8,2,128]{4,3,2,1,0:T(2,128)S(1)}, f32[1,8,8,2,128]{4,3,2,1,0:T(2,128)}, u32[]{:S(2)}) copy-start(f32[1,8,8,2,128]{4,3,2,1,0:T(2,128)} %param.8) | copy-start | bytes 196612

commit v2 on v0

v2 whole, which is shorter than its diff:
```python
import functools

import jax
import jax.numpy as jnp
import numpy as np
from jax import lax
from jax.experimental import pallas as pl
from jax.experimental.pallas import tpu as pltpu
from jax.sharding import PartitionSpec as P

NP = 8
SECTIONS = 4
ZONES = 32
SUB = 8

PENALTY_SPEED = 4.0
TIME_STEP = 0.0005
SPEED_FLOOR = 0.01
MESH = pl.DeviceIdType.MESH
EAST, WEST, NORTH, SOUTH = range(4)
DIRECT = 32


def node_tables():
    points = -np.cos(np.pi * np.arange(NP) / (NP - 1))
    identity = np.eye(NP)
    differ = points[:, None] - points[None, :] + identity
    barycentric = 1.0 / np.prod(differ, axis=1)
    derivative = barycentric[None, :] / barycentric[:, None] / differ * (1.0 - identity)
    derivative = derivative - identity * derivative.sum(axis=1)[:, None]
    order = NP - 1
    end_weight = 1.0 / (order * order)
    return (derivative, float(1.0 / end_weight))


def along_first(table, slabs):
    half = NP // 2
    even = [slabs[k] + slabs[NP - 1 - k] for k in range(half)]
    odd = [slabs[k] - slabs[NP - 1 - k] for k in range(half)]
    out = [None] * NP
    for a in range(half):
        on_even = sum(float(0.5 * (table[a, k] + table[a, NP - 1 - k])) * even[k] for k in range(half))
        on_odd = sum(float(0.5 * (table[a, k] - table[a, NP - 1 - k])) * odd[k] for k in range(half))
        out[a] = on_odd + on_even
        out[NP - 1 - a] = on_odd - on_even
    return out


def kernel(
    axes, ext_x, events,
    depth_hbm, mom_hbm, weight_hbm, wet_hbm, zone_hbm, manning_hbm,
    adj_hbm, grad_ref,
    adj_ref, out_sem, mom_ref, weight_ref, wet_ref, zone_ref, manning_ref, in_sem,
    state, vel_x, vel_y, inv_h, drag_r, flux_x, flux_y, tend, acc, final_adj, later,
    wet_rows, rough_rows, coef_y, zone_acc,
    xs, xr, ys, yr, zs, zr, send_sem, recv_sem, zsend_sem, zrecv_sem,
):
    table, lift = node_tables()
    n_tx, n_ty, n_ev = axes["tx"], axes["ty"], axes["ev"]
    tx, ty, ev = lax.axis_index("tx"), lax.axis_index("ty"), lax.axis_index("ev")
    ext_y = depth_hbm.shape[-1]
    groups = ext_x
    step = ext_x
    per = SUB // ext_x
    blocks = NP // per
    order = [0, NP - 1] + list(range(1, NP - 1))
    order = order if per >= 2 else list(range(NP))
    edge_i = (0, NP - 1)
    has = {EAST: tx < n_tx - 1, WEST: tx > 0, NORTH: ty < n_ty - 1, SOUTH: ty > 0}
    target = {EAST: {"tx": tx + 1}, WEST: {"tx": tx - 1}, NORTH: {"ty": ty + 1}, SOUTH: {"ty": ty - 1}}
    opposite = {EAST: WEST, WEST: EAST, NORTH: SOUTH, SOUTH: NORTH}

    arrive = [
        pltpu.make_async_copy(source, target_ref, in_sem.at[n])
        for n, (source, target_ref) in enumerate((
            (zone_hbm, zone_ref), (manning_hbm, manning_ref), (wet_hbm, wet_ref),
            (depth_hbm, state.at[0, 0]), (mom_hbm, mom_ref), (weight_hbm, weight_ref),
        ))
    ]
    for piece in arrive:
        piece.start()

    barrier = pltpu.get_barrier_semaphore()
    sizes = {"ty": n_ty, "ev": n_ev, "tx": n_tx}
    all_names = ("ty", "ev", "tx")
    direct = n_ty * n_ev * n_tx <= DIRECT
    phases = []
    slots = 0
    for names in ((all_names,) if direct else (all_names[:2], all_names[2:])):
        count = int(np.prod([sizes[name] for name in names]))
        here = 0
        for name in names:
            here = here * sizes[name] + lax.axis_index(name)
        peers = []
        for k in range(1, count):
            rest = lax.rem(here + k, count)
            peer = {}
            for name in reversed(names):
                peer[name] = lax.rem(rest, sizes[name])
                rest = rest // sizes[name]
            peers.append((slots, peer))
            slots += 1
        phases.append(peers)
    for peers in phases:
        for _, peer in peers:
            pl.semaphore_signal(barrier, inc=1, device_id=peer, device_id_type=MESH)

    sub = lax.broadcasted_iota(jnp.int32, (SUB, ext_y), 0)
    lane = lax.broadcasted_iota(jnp.int32, (SUB, ext_y), 1)
    elem = lax.rem(sub, ext_x)

    def flag(yes):
        return jnp.where(yes, 1, 0)

    zero = jnp.float32(0.0)
    inside = {
        WEST: jnp.where((elem == 0) & (flag(has[WEST]) == 0), zero, lift),
        EAST: jnp.where((elem == ext_x - 1) & (flag(has[EAST]) == 0), zero, lift),
        SOUTH: jnp.where((sub >= ext_x) | ((lane == 0) & (flag(has[SOUTH]) == 0)), zero, lift),
        NORTH: jnp.where((sub < SUB - ext_x) | ((lane == ext_y - 1) & (flag(has[NORTH]) == 0)), zero, lift),
    }
    first_elem = (elem == 0) & (flag(has[WEST]) == 1)
    last_elem = (elem == ext_x - 1) & (flag(has[EAST]) == 1)
    first_lane = (lane == 0) & (flag(has[SOUTH]) == 1)
    last_lane = (lane == ext_y - 1) & (flag(has[NORTH]) == 1)

    def spread(rows):
        out = jnp.broadcast_to(rows[0:1], (SUB, ext_y))
        for e in range(1, ext_x):
            out = jnp.where(elem == e, jnp.broadcast_to(rows[e:e + 1], (SUB, ext_y)), out)
        return out

    for t, mat in enumerate((table, table.T)):
        for g in range(groups):
            for h in range(groups):
                for k in range(SUB // step):
                    column = jnp.zeros((SUB, ext_y), jnp.float32)
                    for r in range(SUB):
                        a = (SUB * g + r) // ext_x
                        b = (SUB * h + (r - k * step) % SUB) // ext_x
                        column = jnp.where(sub == r, jnp.float32(-mat[a, b]), column)
                    coef_y[t, g, h, k] = column
    for piece in arrive[:3]:
        piece.wait()
    for s in range(SECTIONS):
        wet_rows[s] = spread(wet_ref[s].astype(jnp.float32))
    zone = spread(zone_ref[...])
    rough = jnp.zeros((SUB, ext_y), jnp.float32)
    for z in range(ZONES):
        rough = jnp.where(zone == z, manning_ref[z], rough)
    rough_rows[...] = rough

    zone_acc[...] = jnp.zeros((SUB, ext_y), jnp.float32)

    def rows(g):
        return pl.ds(SUB * g, SUB)

    def roll(value, shift, axis):
        size = value.shape[axis]
        shift = shift % size
        return value if shift == 0 else pltpu.roll(value, shift, axis)

    def load_coef(t):
        return [[[coef_y[t, g, h, k] for k in range(per)] for h in range(groups)] for g in range(groups)]

    def minus_along_second(coef, source):
        turned = [[roll(source[h], k * step, 0) for k in range(per)] for h in range(groups)]
        return [
            sum(coef[g][h][k] * turned[h][k] for h in range(groups) for k in range(per))
            for g in range(groups)
        ]

    def copy(rnd, side, blk=None):
        if side in (EAST, WEST):
            source, there, sem = xs.at[rnd, side], xr.at[rnd, side], side
        else:
            source, there = ys.at[rnd, side - 2, blk], yr.at[rnd, side - 2, blk]
            sem = 2 + (side - 2) * blocks + blk
        return pltpu.make_async_remote_copy(
            src_ref=source,
            dst_ref=there,
            send_sem=send_sem.at[rnd, sem],
            recv_sem=recv_sem.at[rnd, sem],
            device_id=target[side],
            device_id_type=MESH,
        )

    def start(rnd, sides, blk=None):
        for side in sides:
            @pl.when(has[side])
            def _():
                copy(rnd, side, blk).start()

    def await_from(rnd, sides, blk=None):
        for side in sides:
            @pl.when(has[opposite[side]])
            def _():
                copy(rnd, side, blk).wait_recv()

    def pack_x(rnd, c, east, west):
        to_east, to_west = east[0], west[0]
        for g in range(1, groups):
            to_east = jnp.where(elem == ext_x - 1 - g, roll(east[g], -g, 0), to_east)
            to_west = jnp.where(elem == g, roll(west[g], g, 0), to_west)
        xs[rnd, EAST, c] = to_east
        xs[rnd, WEST, c] = to_west

    def beside_x(rnd, c, g, east, west):
        from_west, from_east = xr[rnd, EAST, c], xr[rnd, WEST, c]
        at_west = jnp.where(first_elem, roll(from_west, -(ext_x - 1 - g), 0), roll(east[g], 1, 0))
        at_east = jnp.where(last_elem, roll(from_east, ext_x - 1 - g, 0), roll(west[g], -1, 0))
        return at_west, at_east

    slot_of = sub // ext_x

    def pack_y(rnd, c, blk, north, south):
        to_north, to_south = roll(north[0], ext_x, 0), south[0]
        for k in range(1, per):
            to_north = jnp.where(slot_of == k, roll(north[k], (k + 1) * ext_x, 0), to_north)
            to_south = jnp.where(slot_of == k, roll(south[k], k * ext_x, 0), to_south)
        ys[rnd, 0, blk, c] = roll(to_north, 1, 1)
        ys[rnd, 1, blk, c] = roll(to_south, -1, 1)

    def beside_y(rnd, c, i):
        blk, k = divmod(order.index(i), per)
        at_south = jnp.where(first_lane, yr[rnd, 0, blk, c], ys[rnd, 0, blk, c])
        at_north = jnp.where(last_lane, yr[rnd, 1, blk, c], ys[rnd, 1, blk, c])
        return roll(at_south, -k * ext_x, 0), roll(at_north, -(k + 1) * ext_x, 0)

    first, last = 0, groups - 1
    comps = range(3)
    pen = 0.5 * PENALTY_SPEED

    def put_fluxes(s, i):
        for g in range(groups):
            h, p, m = (state[s, c, i, rows(g)] for c in comps)
            ih = 1.0 / h
            u, v = p * ih, m * ih
            inv_h[s, i, rows(g)] = ih
            vel_x[s, i, rows(g)] = u
            vel_y[s, i, rows(g)] = v
            pressure = 0.5 * h * h
            cross = p * v
            fx = (p, p * u + pressure, cross)
            fy = (m, cross, m * v + pressure)
            for c in comps:
                flux_x[c, i, rows(g)] = fx[c]
                flux_y[c, i, rows(g)] = fy[c]
            if g == last:
                north = [0.5 * fy[c] + pen * q for c, q in enumerate((h, p, m))]
            if g == first:
                south = [pen * q - 0.5 * fy[c] for c, q in enumerate((h, p, m))]
        return north, south

    def run_columns(rnd, arrived, one_column, x_pack):
        faces = {}
        sweep = list(range(blocks))
        if arrived is not None:
            sweep = sweep[::-1]
        edge_sweep = [blk for blk in sweep if blk in edge_blocks]
        for blk in sweep:
            members = order[blk * per:(blk + 1) * per]
            inner = [i for i in members if i not in edge_i]
            edge = [i for i in members if i in edge_i]
            if arrived is not None:
                await_from(arrived, (NORTH, SOUTH), blk)
                for i in inner:
                    faces[i] = one_column(i)
                if blk == edge_sweep[0]:
                    await_from(arrived, (EAST, WEST))
            for i in edge:
                faces[i] = one_column(i)
            if rnd is not None and blk == edge_sweep[-1]:
                x_pack()
                start(rnd, (EAST, WEST))
            if arrived is None:
                for i in inner:
                    faces[i] = one_column(i)
            if rnd is not None:
                for c in comps:
                    pack_y(rnd, c, blk, [faces[i][0][c] for i in members], [faces[i][1][c] for i in members])
                start(rnd, (NORTH, SOUTH), blk)

    edge_blocks = sorted({order.index(i) // per for i in edge_i})

    def x_traces(s, c):
        east = [0.5 * flux_x[c, NP - 1, rows(g)] + pen * state[s, c, NP - 1, rows(g)] for g in range(groups)]
        west = [pen * state[s, c, 0, rows(g)] - 0.5 * flux_x[c, 0, rows(g)] for g in range(groups)]
        return east, west

    coefs = (0.5 * TIME_STEP, 0.5 * TIME_STEP, TIME_STEP)
    sums = (1.0, 2.0, 2.0, 1.0)
    final_weights = (TIME_STEP / 6.0, TIME_STEP / 3.0, TIME_STEP / 3.0, TIME_STEP / 6.0)

    def pack_forward(s):
        for c in comps:
            pack_x(s, c, *x_traces(s, c))

    def pack_back(rnd):
        for c in comps:
            pack_x(rnd, c, *cot_faces(c))

    def cot_faces(c):
        return (
            [acc[c, NP - 1, rows(g)] for g in range(groups)],
            [acc[c, 0, rows(g)] for g in range(groups)],
        )

    def set_up(i):
        state[0, 1, i] = mom_ref[0, i]
        state[0, 2, i] = mom_ref[1, i]
        return put_fluxes(0, i)

    for piece in arrive[3:]:
        piece.wait()
    pl.semaphore_wait(barrier, slots)
    run_columns(0, None, set_up, lambda: pack_forward(0))

    for s in range(SECTIONS):
        def volume(blk, _):
            coef = load_coef(0)
            rough_g = rough_rows[...]
            for n in range(per):
                i = blk * per + n
                out = [minus_along_second(coef, [flux_y[c, i, rows(g)] for g in range(groups)]) for c in comps]
                for g in range(groups):
                    h, p, m = (state[s, c, i, rows(g)] for c in comps)
                    u, v = vel_x[s, i, rows(g)], vel_y[s, i, rows(g)]
                    speed = jnp.sqrt(u * u + v * v + SPEED_FLOOR)
                    kr = rough_g * speed * jnp.exp((-4.0 / 3.0) * jnp.log(h))
                    drag_r[s, i, rows(g)] = kr
                    k = rough_g * kr
                    tend[0, i, rows(g)] = out[0][g]
                    tend[1, i, rows(g)] = out[1][g] - k * p
                    tend[2, i, rows(g)] = out[2][g] - k * m
            return _

        lax.fori_loop(0, blocks, volume, 0)

        def volume_x(c, _):
            for g in range(groups):
                out = along_first(table, [flux_x[c, i, rows(g)] for i in range(NP)])
                for i in range(NP):
                    tend[c, i, rows(g)] -= out[i]
            return _

        lax.fori_loop(0, 3, volume_x, 0)

        def finish(i):
            wet = wet_rows[s]
            for c in comps:
                at_south, at_north = beside_y(s, c, i)
                for g in range(groups):
                    slope = tend[c, i, rows(g)]
                    q = state[s, c, i, rows(g)]
                    if i in edge_i:
                        at_west, at_east = beside_x(s, c, g, *old_x[c])
                        if i == 0:
                            slope = slope + inside[WEST] * (at_west - (0.5 * flux_x[c, i, rows(g)] + pen * q))
                        else:
                            slope = slope + inside[EAST] * (at_east - (pen * q - 0.5 * flux_x[c, i, rows(g)]))
                    if g == first:
                        slope = slope + inside[SOUTH] * (at_south - (0.5 * flux_y[c, i, rows(g)] + pen * q))
                    if g == last:
                        slope = slope + inside[NORTH] * (at_north - (pen * q - 0.5 * flux_y[c, i, rows(g)]))
                    slope = wet * slope
                    start_q = state[0, c, i, rows(g)]
                    if s == 0:
                        acc[c, i, rows(g)] = slope
                    elif s < SECTIONS - 1:
                        acc[c, i, rows(g)] += sums[s] * slope
                    if s < SECTIONS - 1:
                        state[s + 1, c, i, rows(g)] = start_q + coefs[s] * slope
                    elif c > 0:
                        total = acc[c, i, rows(g)] + slope
                        final = start_q + (TIME_STEP / 6.0) * total
                        seed = weight_ref[i, rows(g)] * final
                        final_adj[c - 1, i, rows(g)] = seed
                        adj_ref[c, i, rows(g)] = seed
                    else:
                        adj_ref[c, i, rows(g)] = jnp.zeros((SUB, ext_y), jnp.float32)
            if s < SECTIONS - 1:
                return put_fluxes(s + 1, i)
            return put_cot(s, i)

        def put_cot(s, i):
            wet = wet_rows[s]
            north, south = [], []
            for c in comps:
                for g in range(groups):
                    value = None
                    if c > 0:
                        value = final_weights[s] * final_adj[c - 1, i, rows(g)]
                    if s < SECTIONS - 1:
                        back = coefs[s] * later[c, i, rows(g)]
                        value = back if value is None else value + back
                    if value is None:
                        value = jnp.zeros((SUB, ext_y), jnp.float32)
                    value = wet * value
                    acc[c, i, rows(g)] = value
                    if g == last:
                        north.append(value)
                    if g == first:
                        south.append(value)
            return north, south

        old_x = [x_traces(s, c) for c in comps]
        if s < SECTIONS - 1:
            run_columns(s + 1, s, finish, lambda: pack_forward(s + 1))
        else:
            run_columns(SECTIONS, s, finish, lambda: pack_back(SECTIONS))

    def zone_copy(n, slot, peer):
        return pltpu.make_async_remote_copy(
            src_ref=zs.at[n], dst_ref=zr.at[slot],
            send_sem=zsend_sem.at[slot], recv_sem=zrecv_sem.at[slot],
            device_id=peer, device_id_type=MESH,
        )

    def zone_start(n):
        for slot, peer in phases[n]:
            zone_copy(n, slot, peer).start()

    def zone_end(n):
        total = zs[n]
        for slot, peer in phases[n]:
            zone_copy(n, slot, peer).wait_recv()
            total = total + zr[slot]
        return total

    def write_out(n, c, first_i, count):
        part = pl.ds(first_i, count)
        return pltpu.make_async_copy(adj_ref.at[c, part], adj_hbm.at[c, part], out_sem.at[n, c])

    for s in reversed(range(SECTIONS)):
        rnd = 2 * SECTIONS - 1 - s
        def drag_back(blk, _):
            rough_g = rough_rows[...]
            parts = []
            for n in range(per):
                i = blk * per + n
                for g in range(groups):
                    h, p, m = (state[s, c, i, rows(g)] for c in comps)
                    u, v, ih = vel_x[s, i, rows(g)], vel_y[s, i, rows(g)], inv_h[s, i, rows(g)]
                    kr = drag_r[s, i, rows(g)]
                    c1, c2 = acc[1, i, rows(g)], acc[2, i, rows(g)]
                    part = kr * (c1 * p + c2 * m)
                    parts.append(part)
                    k = rough_g * kr
                    e = rough_g * part * ih
                    square = u * u + v * v
                    eq = e / (square + SPEED_FLOOR)
                    tend[0, i, rows(g)] = (4.0 / 3.0) * e + eq * square
                    tend[1, i, rows(g)] = -(k * c1 + eq * u)
                    tend[2, i, rows(g)] = -(k * c2 + eq * v)
            zone_acc[...] += sum(parts)
            return _

        lax.fori_loop(0, blocks, drag_back, 0)

        if s == 0:
            total = zone_acc[...]
            shift = ext_x
            while shift < SUB:
                total = total + roll(total, shift, 0)
                shift *= 2
            total = -2.0 * total
            zones = lax.broadcasted_iota(jnp.int32, (ZONES, ext_y), 0)
            spot = jnp.zeros((ZONES, ext_y), jnp.float32)
            for e in range(ext_x):
                ids = jnp.broadcast_to(zone_ref[e:e + 1, :], (ZONES, ext_y))
                spot = spot + jnp.where(ids == zones, jnp.broadcast_to(total[e:e + 1], (ZONES, ext_y)), 0.0)
            per_zone = jnp.sum(spot, axis=1, keepdims=True)
            spots = lax.broadcasted_iota(jnp.int32, (ZONES, ext_y), 1)
            line = jnp.sum(jnp.where(zones == spots, jnp.broadcast_to(per_zone, (ZONES, ext_y)), 0.0), axis=0, keepdims=True)
            zs[0] = line
            zone_start(0)

        def volume_y(blk, _):
            coef = load_coef(1)
            for n in range(per):
                i = blk * per + n
                for c in comps:
                    out = minus_along_second(coef, [acc[c, i, rows(g)] for g in range(groups)])
                    for g in range(groups):
                        flux_y[c, i, rows(g)] = out[g]
            return _

        lax.fori_loop(0, blocks, volume_y, 0)

        def volume_back(c, _):
            for g in range(groups):
                out = along_first(-table.T, [acc[c, i, rows(g)] for i in range(NP)])
                for i in range(NP):
                    flux_x[c, i, rows(g)] = out[i]
            return _

        lax.fori_loop(0, 3, volume_back, 0)

        old_x = [cot_faces(c) for c in comps]

        def finish_back(i):
            s_in, n_in, w_in, e_in = inside[SOUTH], inside[NORTH], inside[WEST], inside[EAST]
            beside = [beside_y(rnd, c, i) for c in comps]
            for g in range(groups):
                a = [flux_x[c, i, rows(g)] for c in comps]
                b = [flux_y[c, i, rows(g)] for c in comps]
                out = [tend[c, i, rows(g)] for c in comps]
                own = [acc[c, i, rows(g)] for c in comps]
                for c in comps:
                    if i in edge_i:
                        at_west, at_east = beside_x(rnd, c, g, *old_x[c])
                        if i == 0:
                            a[c] = a[c] - (0.5 * w_in) * (own[c] + at_west)
                            out[c] = out[c] + (pen * w_in) * (at_west - own[c])
                        else:
                            a[c] = a[c] + (0.5 * e_in) * (own[c] + at_east)
                            out[c] = out[c] + (pen * e_in) * (at_east - own[c])
                    if g == first:
                        there = beside[c][0]
                        b[c] = b[c] - (0.5 * s_in) * (own[c] + there)
                        out[c] = out[c] + (pen * s_in) * (there - own[c])
                    if g == last:
                        there = beside[c][1]
                        b[c] = b[c] + (0.5 * n_in) * (own[c] + there)
                        out[c] = out[c] + (pen * n_in) * (there - own[c])
                h = state[s, 0, i, rows(g)]
                u, v = vel_x[s, i, rows(g)], vel_y[s, i, rows(g)]
                cross = a[2] + b[1]
                au, bv = a[1] * u, b[2] * v
                cot = (
                    out[0] + (a[1] + b[2]) * h - au * u - bv * v - cross * (u * v),
                    out[1] + a[0] + 2.0 * au + cross * v,
                    out[2] + b[0] + 2.0 * bv + cross * u,
                )
                for c in comps:
                    adj_ref[c, i, rows(g)] += cot[c]
                    if s > 0:
                        later[c, i, rows(g)] = cot[c]
            if s > 0:
                return put_cot(s - 1, i)

        if s > 0:
            run_columns(rnd + 1, rnd, finish_back, lambda: pack_back(rnd + 1))
        else:
            run_columns(None, rnd, finish_back, None)

    writes = [write_out(0, c, 0, NP) for c in comps]
    for write in writes:
        write.start()
    whole = zone_end(0)
    if not direct:
        zs[1] = whole
        zone_start(1)
        whole = zone_end(1)
    nodes = events * n_ev * ext_x * n_tx * ext_y * n_ty * NP * NP
    grad_ref[...] = whole[:, :ZONES] * (ZONES / (TIME_STEP * nodes))

    for rnd in range(2 * SECTIONS):
        for side in (EAST, WEST):
            @pl.when(has[side])
            def _():
                copy(rnd, side).wait_send()
        for side in (NORTH, SOUTH):
            @pl.when(has[side])
            def _():
                for blk in range(blocks):
                    copy(rnd, side, blk).wait_send()
    for n, peers in enumerate(phases):
        for slot, peer in peers:
            zone_copy(n, slot, peer).wait_send()
    for write in writes:
        write.wait()


def local(axes, depth0, momentum0, obs_weight, wet_mask, zone_id, manning):
    ext_x, ext_y = depth0.shape[3:]
    rows = NP * ext_x
    field = (NP, rows, ext_y)
    rounds = 2 * SECTIONS
    slots = axes["ty"] * axes["ev"] * axes["tx"]
    if slots > DIRECT:
        slots = axes["ty"] * axes["ev"] + axes["tx"]
    f32 = jnp.float32
    vmem = pl.BlockSpec(memory_space=pltpu.VMEM)
    adjoint, grad = pl.pallas_call(
        functools.partial(kernel, axes, ext_x, depth0.shape[0]),
        out_shape=(
            jax.ShapeDtypeStruct((3,) + field, f32),
            jax.ShapeDtypeStruct((1, ZONES), f32),
        ),
        in_specs=[pl.BlockSpec(memory_space=pltpu.HBM)] * 6,
        out_specs=(pl.BlockSpec(memory_space=pltpu.HBM), vmem),
        scratch_shapes=[
            pltpu.VMEM((3,) + field, f32),
            pltpu.SemaphoreType.DMA((1, 3)),
            pltpu.VMEM((2,) + field, f32),
            pltpu.VMEM(field, f32),
            pltpu.VMEM(wet_mask.shape[1:], jnp.int32),
            pltpu.VMEM(zone_id.shape, jnp.int32),
            pltpu.SMEM(manning.shape, f32),
            pltpu.SemaphoreType.DMA((6,)),
            pltpu.VMEM((SECTIONS, 3) + field, f32),
            pltpu.VMEM((SECTIONS,) + field, f32),
            pltpu.VMEM((SECTIONS,) + field, f32),
            pltpu.VMEM((SECTIONS,) + field, f32),
            pltpu.VMEM((SECTIONS,) + field, f32),
            pltpu.VMEM((3,) + field, f32),
            pltpu.VMEM((3,) + field, f32),
            pltpu.VMEM((3,) + field, f32),
            pltpu.VMEM((3,) + field, f32),
            pltpu.VMEM((2,) + field, f32),
            pltpu.VMEM((3,) + field, f32),
            pltpu.VMEM((SECTIONS, SUB, ext_y), f32),
            pltpu.VMEM((SUB, ext_y), f32),
            pltpu.VMEM((2, ext_x, ext_x, SUB // ext_x, SUB, ext_y), f32),
            pltpu.VMEM((SUB, ext_y), f32),
            pltpu.VMEM((rounds, 2, 3, SUB, ext_y), f32),
            pltpu.VMEM((rounds, 2, 3, SUB, ext_y), f32),
            pltpu.VMEM((rounds, 2, NP // (SUB // ext_x), 3, SUB, ext_y), f32),
            pltpu.VMEM((rounds, 2, NP // (SUB // ext_x), 3, SUB, ext_y), f32),
            pltpu.VMEM((2, 1, ext_y), f32),
            pltpu.VMEM((slots, 1, ext_y), f32),
            pltpu.SemaphoreType.DMA((rounds, 2 + 2 * (NP // (SUB // ext_x)))),
            pltpu.SemaphoreType.DMA((rounds, 2 + 2 * (NP // (SUB // ext_x)))),
            pltpu.SemaphoreType.DMA((slots,)),
            pltpu.SemaphoreType.DMA((slots,)),
        ],
        compiler_params=pltpu.CompilerParams(
            collective_id=0, has_side_effects=True, vmem_limit_bytes=60 * 1024 * 1024
        ),
    )(
        depth0.reshape(field),
        momentum0.reshape((2,) + field),
        obs_weight.reshape(field),
        wet_mask.reshape(wet_mask.shape[1:]),
        zone_id,
        manning,
    )
    return adjoint.reshape((1, 3, NP, NP, ext_x, ext_y)), grad.reshape((ZONES,))


def solution(mesh):
    in_specs = (
        P(("basin", "ev"), None, None, "tx", "ty"),
        P(("basin", "ev"), None, None, None, "tx", "ty"),
        P(("basin", "ev"), None, None, "tx", "ty"),
        P(("basin", "ev"), None, "tx", "ty"),
        P(("basin", "tx"), "ty"),
        P("basin"),
    )
    out_specs = (P(("basin", "ev"), None, None, None, "tx", "ty"), P("basin"))
    return jax.shard_map(
        functools.partial(local, dict(mesh.shape)),
        mesh=mesh, in_specs=in_specs, out_specs=out_specs, check_vma=False,
    )
```

time: 42.9 us -> 34 us (0.79)
  Pallas kernels: 37.5 us -> 31.1 us
  local copies, waits for them, and re-layouts: 4.45 us -> 2.13 us
    pallas_call x1, Pallas kernels: 37.5 us -> 31.1 us  [local(): pl.pallas_call(functools.partial(kernel, axes, ext_x, depth0.shape[0]), o...]
    unnamed x14 -> x4, local copies, waits for them, and re-layouts: 4.45 us -> 2.13 us
where the time goes in v2:
time: 34 us; the launch traced here: 33.8 us
  Pallas kernels  31.1 us (91%)
  local copies, waits for them, and re-layouts  2.13 us (6%)
  between operations  0.65 us (2%)
    pallas_call x1, Pallas kernels, local(): pl.pallas_call(functools.partial(kernel, axes, ext_x, depth0.shape[0]), o...  31.1 us
    unnamed x4, local copies, waits for them, and re-layouts  2.13 us

profile of v2, /device:TPU:0, one launch (start us, length us, event | category | flops | bytes accessed | tf_op | source)
XLA Modules:
  0.0 33.8 jit_solution(7125096860184415408)
XLA Ops:
  0.6 31.1 %shard_map.77 = (f32[3,8,16,128]{3,2,1,0:T(8,128)}, f32[1,32]{1,0:T(1,128)}) custom-call(f32[8,16,128]{2,1,0:T(8,128)} %bitcast.8, f32[2,8,16,128]{3,2,1,0:T(8,128)} %bitcast.7, f32[8,16,128]{2,1,0:T(8,128)} %bitcast.9, s32[4,2,128]{2,1,0:T(2,128)} %bitcast.10, s32[2,128]{1,0:T(2,128)} %zone_hbm.1, f32[32]{0:T(128)} %manning_hbm.1), custom_call_target="tpu_custom_call" | custom-call | tf_op jit(solution)/shard_map/pallas_call | solution.py:586
  31.7 0.0 copy-start
  31.7 1.6 %copy.10 = f32[1,3,8,8,2,128]{5,4,3,2,1,0:T(2,128)} copy(f32[1,3,8,8,2,128]{5,4,3,2,1,0:T(2,128)} %bitcast.6) | data formatting | bytes 393216
  33.3 0.0 copy-done
  33.3 0.5 %copy.11 = f32[32]{0:T(128)} copy(f32[32]{0:T(128)S(1)} %bitcast.11) | data formatting | bytes 256
Async XLA Ops:
  31.7 1.6 %copy-start = (f32[1,32]{1,0:T(1,128)S(1)}, f32[1,32]{1,0:T(1,128)}, u32[]{:S(2)}) copy-start(f32[1,32]{1,0:T(1,128)} %get-tuple-element.5) | copy-start | bytes 388

commit v3 on v2

--- a/solution.py
+++ b/solution.py
@@ -170,32 +170,58 @@
             for g in range(groups)
         ]
 
+    pair = n_ty == 2
+    beyond = 1 - ty
+
     def copy(rnd, side, blk=None):
         if side in (EAST, WEST):
-            source, there, sem = xs.at[rnd, side], xr.at[rnd, side], side
+            source, there, sem, device = xs.at[rnd, side], xr.at[rnd, side], side, target[side]
+        elif side is None:
+            source, there = ys.at[rnd, ty, blk], yr.at[rnd, ty, blk]
+            sem, device = 2 + blk, {"ty": beyond}
         else:
             source, there = ys.at[rnd, side - 2, blk], yr.at[rnd, side - 2, blk]
-            sem = 2 + (side - 2) * blocks + blk
+            sem, device = 2 + (side - 2) * blocks + blk, target[side]
         return pltpu.make_async_remote_copy(
             src_ref=source,
             dst_ref=there,
             send_sem=send_sem.at[rnd, sem],
             recv_sem=recv_sem.at[rnd, sem],
-            device_id=target[side],
+            device_id=device,
             device_id_type=MESH,
         )
 
     def start(rnd, sides, blk=None):
+        if pair and NORTH in sides:
+            copy(rnd, None, blk).start()
+            return
         for side in sides:
             @pl.when(has[side])
             def _():
                 copy(rnd, side, blk).start()
 
     def await_from(rnd, sides, blk=None):
+        if pair and NORTH in sides:
+            copy(rnd, None, blk).wait_recv()
+            return
         for side in sides:
             @pl.when(has[opposite[side]])
             def _():
                 copy(rnd, side, blk).wait_recv()
+
+    def end_sends(rnd):
+        for side in (EAST, WEST):
+            @pl.when(has[side])
+            def _():
+                copy(rnd, side).wait_send()
+        for blk in range(blocks):
+            if pair:
+                copy(rnd, None, blk).wait_send()
+                continue
+            for side in (NORTH, SOUTH):
+                @pl.when(has[side])
+                def _():
+                    copy(rnd, side, blk).wait_send()
 
     def pack_x(rnd, c, east, west):
         to_east, to_west = east[0], west[0]
@@ -335,7 +361,7 @@
                     tend[2, i, rows(g)] = out[2][g] - k * m
             return _
 
-        lax.fori_loop(0, blocks, volume, 0)
+        lax.fori_loop(0, blocks, volume, 0, unroll=True)
 
         def volume_x(c, _):
             for g in range(groups):
@@ -344,7 +370,9 @@
                     tend[c, i, rows(g)] -= out[i]
             return _
 
-        lax.fori_loop(0, 3, volume_x, 0)
+        lax.fori_loop(0, 3, volume_x, 0, unroll=True)
+        if s > 0:
+            end_sends(s - 1)
 
         def finish(i):
             wet = wet_rows[s]
@@ -413,7 +441,7 @@
     def zone_copy(n, slot, peer):
         return pltpu.make_async_remote_copy(
             src_ref=zs.at[n], dst_ref=zr.at[slot],
-            send_sem=zsend_sem.at[slot], recv_sem=zrecv_sem.at[slot],
+            send_sem=zsend_sem.at[slot], recv_sem=zrecv_sem.at[n],
             device_id=peer, device_id_type=MESH,
         )
 
@@ -422,9 +450,12 @@
             zone_copy(n, slot, peer).start()
 
     def zone_end(n):
+        if not phases[n]:
+            return zs[n]
+        part = zr.at[pl.ds(phases[n][0][0], len(phases[n]))]
+        pltpu.make_async_copy(part, part, zrecv_sem.at[n]).wait()
         total = zs[n]
-        for slot, peer in phases[n]:
-            zone_copy(n, slot, peer).wait_recv()
+        for slot, _ in phases[n]:
             total = total + zr[slot]
         return total
 
@@ -456,7 +487,7 @@
             zone_acc[...] += sum(parts)
             return _
 
-        lax.fori_loop(0, blocks, drag_back, 0)
+        lax.fori_loop(0, blocks, drag_back, 0, unroll=True)
 
         if s == 0:
             total = zone_acc[...]
@@ -486,7 +517,7 @@
                         flux_y[c, i, rows(g)] = out[g]
             return _
 
-        lax.fori_loop(0, blocks, volume_y, 0)
+        lax.fori_loop(0, blocks, volume_y, 0, unroll=True)
 
         def volume_back(c, _):
             for g in range(groups):
@@ -495,7 +526,8 @@
                     flux_x[c, i, rows(g)] = out[i]
             return _
 
-        lax.fori_loop(0, 3, volume_back, 0)
+        lax.fori_loop(0, 3, volume_back, 0, unroll=True)
+        end_sends(rnd - 1)
 
         old_x = [cot_faces(c) for c in comps]
 
@@ -556,21 +588,21 @@
     nodes = events * n_ev * ext_x * n_tx * ext_y * n_ty * NP * NP
     grad_ref[...] = whole[:, :ZONES] * (ZONES / (TIME_STEP * nodes))
 
-    for rnd in range(2 * SECTIONS):
-        for side in (EAST, WEST):
-            @pl.when(has[side])
-            def _():
-                copy(rnd, side).wait_send()
-        for side in (NORTH, SOUTH):
-            @pl.when(has[side])
-            def _():
-                for blk in range(blocks):
-                    copy(rnd, side, blk).wait_send()
+    end_sends(2 * SECTIONS - 1)
     for n, peers in enumerate(phases):
         for slot, peer in peers:
             zone_copy(n, slot, peer).wait_send()
     for write in writes:
         write.wait()
+
+
+def hand_over(adjoint_ref, grad_ref, adjoint_out, grad_out, sem):
+    moves = [pltpu.make_async_copy(adjoint_ref.at[c], adjoint_out.at[c], sem.at[c]) for c in range(3)]
+    moves.append(pltpu.make_async_copy(grad_ref, grad_out, sem.at[3]))
+    for move in moves:
+        move.start()
+    for move in moves:
+        move.wait()
 
 
 def local(axes, depth0, momentum0, obs_weight, wet_mask, zone_id, manning):
@@ -637,6 +669,17 @@
         zone_id,
         manning,
     )
+    anywhere = pl.BlockSpec(memory_space=pl.ANY)
+    adjoint, grad = pl.pallas_call(
+        hand_over,
+        out_shape=(
+            jax.ShapeDtypeStruct(adjoint.shape, f32),
+            jax.ShapeDtypeStruct(grad.shape, f32),
+        ),
+        in_specs=[anywhere] * 2,
+        out_specs=(anywhere, anywhere),
+        scratch_shapes=[pltpu.SemaphoreType.DMA((4,))],
+    )(adjoint, grad)
     return adjoint.reshape((1, 3, NP, NP, ext_x, ext_y)), grad.reshape((ZONES,))
 
 

time: 34 us -> 38.9 us (1.14)
  Pallas kernels: 31.1 us -> 38.1 us
  local copies, waits for them, and re-layouts: 2.13 us -> 0 us
    pallas_call x0 -> x1, Pallas kernels: none -> 7.11 us  [local(): pl.pallas_call(hand_over, out_shape=(jax.ShapeDtypeStruct(adjoint.shape,...]
    unnamed x4 -> x0, local copies, waits for them, and re-layouts: 2.13 us -> none
where the time goes in v3:
time: 38.9 us; the launch traced here: 38.7 us
  Pallas kernels  38.1 us (98%)
  between operations  0.64 us (2%)
    pallas_call x1, Pallas kernels, local(): pl.pallas_call(functools.partial(kernel, axes, ext_x, depth0.shape[0]), o...  31 us
    pallas_call x1, Pallas kernels, local(): pl.pallas_call(hand_over, out_shape=(jax.ShapeDtypeStruct(adjoint.shape,...  7.11 us

profile of v3, /device:TPU:0, one launch (start us, length us, event | category | flops | bytes accessed | tf_op | source)
XLA Modules:
  0.0 38.7 jit_solution(17857084373304943460)
XLA Ops:
  0.6 31.0 %shard_map.77 = (f32[3,8,16,128]{3,2,1,0:T(8,128)}, f32[1,32]{1,0:T(1,128)}) custom-call(f32[8,16,128]{2,1,0:T(8,128)} %bitcast.7, f32[2,8,16,128]{3,2,1,0:T(8,128)} %bitcast.6, f32[8,16,128]{2,1,0:T(8,128)} %bitcast.8, s32[4,2,128]{2,1,0:T(2,128)} %bitcast.9, s32[2,128]{1,0:T(2,128)} %zone_hbm.1, f32[32]{0:T(128)} %manning_hbm.1), custom_call_target="tpu_custom_call" | custom-call | tf_op jit(solution)/shard_map/pallas_call | solution.py:618
  31.6 7.1 %shard_map.78 = (f32[3,8,16,128]{3,2,1,0:T(8,128)}, f32[1,32]{1,0:T(1,128)}) custom-call(f32[3,8,16,128]{3,2,1,0:T(8,128)} %get-tuple-element.6.adjoint_ref, f32[1,32]{1,0:T(1,128)} %get-tuple-element.7.grad_ref), custom_call_target="tpu_custom_call" | custom-call | tf_op jit(solution)/shard_map/pallas_call | solution.py:673

commit v4 on v3

--- a/solution.py
+++ b/solution.py
@@ -62,10 +62,16 @@
     groups = ext_x
     step = ext_x
     per = SUB // ext_x
+    edge_i = (0, NP - 1)
+    inner_i = tuple(range(1, NP - 1))
     blocks = NP // per
-    order = [0, NP - 1] + list(range(1, NP - 1))
-    order = order if per >= 2 else list(range(NP))
-    edge_i = (0, NP - 1)
+    packs = []
+    spans = []
+    for members in (edge_i, inner_i):
+        first_pack = len(packs)
+        packs += [members[n:n + per] for n in range(0, len(members), per)]
+        spans.append((first_pack, len(packs) - first_pack))
+    parts = len(spans)
     has = {EAST: tx < n_tx - 1, WEST: tx > 0, NORTH: ty < n_ty - 1, SOUTH: ty > 0}
     target = {EAST: {"tx": tx + 1}, WEST: {"tx": tx - 1}, NORTH: {"ty": ty + 1}, SOUTH: {"ty": ty - 1}}
     opposite = {EAST: WEST, WEST: EAST, NORTH: SOUTH, SOUTH: NORTH}
@@ -177,11 +183,13 @@
         if side in (EAST, WEST):
             source, there, sem, device = xs.at[rnd, side], xr.at[rnd, side], side, target[side]
         elif side is None:
-            source, there = ys.at[rnd, ty, blk], yr.at[rnd, ty, blk]
+            span = pl.ds(*spans[blk])
+            source, there = ys.at[rnd, ty, span], yr.at[rnd, ty, span]
             sem, device = 2 + blk, {"ty": beyond}
         else:
-            source, there = ys.at[rnd, side - 2, blk], yr.at[rnd, side - 2, blk]
-            sem, device = 2 + (side - 2) * blocks + blk, target[side]
+            span = pl.ds(*spans[blk])
+            source, there = ys.at[rnd, side - 2, span], yr.at[rnd, side - 2, span]
+            sem, device = 2 + (side - 2) * parts + blk, target[side]
         return pltpu.make_async_remote_copy(
             src_ref=source,
             dst_ref=there,
@@ -214,7 +222,7 @@
             @pl.when(has[side])
             def _():
                 copy(rnd, side).wait_send()
-        for blk in range(blocks):
+        for blk in range(parts):
             if pair:
                 copy(rnd, None, blk).wait_send()
                 continue
@@ -241,14 +249,14 @@
 
     def pack_y(rnd, c, blk, north, south):
         to_north, to_south = roll(north[0], ext_x, 0), south[0]
-        for k in range(1, per):
+        for k in range(1, len(north)):
             to_north = jnp.where(slot_of == k, roll(north[k], (k + 1) * ext_x, 0), to_north)
             to_south = jnp.where(slot_of == k, roll(south[k], k * ext_x, 0), to_south)
         ys[rnd, 0, blk, c] = roll(to_north, 1, 1)
         ys[rnd, 1, blk, c] = roll(to_south, -1, 1)
 
     def beside_y(rnd, c, i):
-        blk, k = divmod(order.index(i), per)
+        blk, k = next((n, m.index(i)) for n, m in enumerate(packs) if i in m)
         at_south = jnp.where(first_lane, yr[rnd, 0, blk, c], ys[rnd, 0, blk, c])
         at_north = jnp.where(last_lane, yr[rnd, 1, blk, c], ys[rnd, 1, blk, c])
         return roll(at_south, -k * ext_x, 0), roll(at_north, -(k + 1) * ext_x, 0)
@@ -279,35 +287,22 @@
         return north, south
 
     def run_columns(rnd, arrived, one_column, x_pack):
-        faces = {}
-        sweep = list(range(blocks))
-        if arrived is not None:
-            sweep = sweep[::-1]
-        edge_sweep = [blk for blk in sweep if blk in edge_blocks]
-        for blk in sweep:
-            members = order[blk * per:(blk + 1) * per]
-            inner = [i for i in members if i not in edge_i]
-            edge = [i for i in members if i in edge_i]
+        for part in ((0, 1) if arrived is None else (1, 0)):
             if arrived is not None:
-                await_from(arrived, (NORTH, SOUTH), blk)
-                for i in inner:
-                    faces[i] = one_column(i)
-                if blk == edge_sweep[0]:
+                await_from(arrived, (NORTH, SOUTH), part)
+                if part == 0:
                     await_from(arrived, (EAST, WEST))
-            for i in edge:
-                faces[i] = one_column(i)
-            if rnd is not None and blk == edge_sweep[-1]:
+            faces = {i: one_column(i) for i in (edge_i, inner_i)[part]}
+            if rnd is None:
+                continue
+            if part == 0:
                 x_pack()
                 start(rnd, (EAST, WEST))
-            if arrived is None:
-                for i in inner:
-                    faces[i] = one_column(i)
-            if rnd is not None:
+            head, count = spans[part]
+            for blk in range(head, head + count):
                 for c in comps:
-                    pack_y(rnd, c, blk, [faces[i][0][c] for i in members], [faces[i][1][c] for i in members])
-                start(rnd, (NORTH, SOUTH), blk)
-
-    edge_blocks = sorted({order.index(i) // per for i in edge_i})
+                    pack_y(rnd, c, blk, [faces[i][0][c] for i in packs[blk]], [faces[i][1][c] for i in packs[blk]])
+            start(rnd, (NORTH, SOUTH), part)
 
     def x_traces(s, c):
         east = [0.5 * flux_x[c, NP - 1, rows(g)] + pen * state[s, c, NP - 1, rows(g)] for g in range(groups)]
@@ -596,12 +591,17 @@
         write.wait()
 
 
-def hand_over(adjoint_ref, grad_ref, adjoint_out, grad_out, sem):
-    moves = [pltpu.make_async_copy(adjoint_ref.at[c], adjoint_out.at[c], sem.at[c]) for c in range(3)]
-    moves.append(pltpu.make_async_copy(grad_ref, grad_out, sem.at[3]))
-    for move in moves:
+def hand_over(adjoint_ref, grad_ref, adjoint_out, grad_out, adjoint_mid, grad_mid, sem):
+    take = [pltpu.make_async_copy(adjoint_ref.at[c], adjoint_mid.at[c], sem.at[c]) for c in range(3)]
+    give = [pltpu.make_async_copy(adjoint_mid.at[c], adjoint_out.at[c], sem.at[4 + c]) for c in range(3)]
+    take.append(pltpu.make_async_copy(grad_ref, grad_mid, sem.at[3]))
+    give.append(pltpu.make_async_copy(grad_mid, grad_out, sem.at[7]))
+    for move in take:
         move.start()
-    for move in moves:
+    for taken, given in zip(take, give):
+        taken.wait()
+        given.start()
+    for move in give:
         move.wait()
 
 
@@ -610,6 +610,7 @@
     rows = NP * ext_x
     field = (NP, rows, ext_y)
     rounds = 2 * SECTIONS
+    packs = pl.cdiv(2 * ext_x, SUB) + pl.cdiv((NP - 2) * ext_x, SUB)
     slots = axes["ty"] * axes["ev"] * axes["tx"]
     if slots > DIRECT:
         slots = axes["ty"] * axes["ev"] + axes["tx"]
@@ -649,12 +650,12 @@
             pltpu.VMEM((SUB, ext_y), f32),
             pltpu.VMEM((rounds, 2, 3, SUB, ext_y), f32),
             pltpu.VMEM((rounds, 2, 3, SUB, ext_y), f32),
-            pltpu.VMEM((rounds, 2, NP // (SUB // ext_x), 3, SUB, ext_y), f32),
-            pltpu.VMEM((rounds, 2, NP // (SUB // ext_x), 3, SUB, ext_y), f32),
+            pltpu.VMEM((rounds, 2, packs, 3, SUB, ext_y), f32),
+            pltpu.VMEM((rounds, 2, packs, 3, SUB, ext_y), f32),
             pltpu.VMEM((2, 1, ext_y), f32),
             pltpu.VMEM((slots, 1, ext_y), f32),
-            pltpu.SemaphoreType.DMA((rounds, 2 + 2 * (NP // (SUB // ext_x)))),
-            pltpu.SemaphoreType.DMA((rounds, 2 + 2 * (NP // (SUB // ext_x)))),
+            pltpu.SemaphoreType.DMA((rounds, 6)),
+            pltpu.SemaphoreType.DMA((rounds, 6)),
             pltpu.SemaphoreType.DMA((slots,)),
             pltpu.SemaphoreType.DMA((slots,)),
         ],
@@ -678,7 +679,11 @@
         ),
         in_specs=[anywhere] * 2,
         out_specs=(anywhere, anywhere),
-        scratch_shapes=[pltpu.SemaphoreType.DMA((4,))],
+        scratch_shapes=[
+            pltpu.VMEM(adjoint.shape, f32),
+            pltpu.VMEM(grad.shape, f32),
+            pltpu.SemaphoreType.DMA((8,)),
+        ],
     )(adjoint, grad)
     return adjoint.reshape((1, 3, NP, NP, ext_x, ext_y)), grad.reshape((ZONES,))
 

time: 38.9 us -> 33.4 us (0.86)
  Pallas kernels: 38.1 us -> 32.6 us
    pallas_call x1, Pallas kernels: 7.11 us -> 1.6 us  [local(): pl.pallas_call(hand_over, out_shape=(jax.ShapeDtypeStruct(adjoint.shape,...]
where the time goes in v4:
time: 33.4 us; the launch traced here: 33.2 us
  Pallas kernels  32.6 us (98%)
  between operations  0.64 us (2%)
    pallas_call x1, Pallas kernels, local(): pl.pallas_call(functools.partial(kernel, axes, ext_x, depth0.shape[0]), o...  31 us
    pallas_call x1, Pallas kernels, local(): pl.pallas_call(hand_over, out_shape=(jax.ShapeDtypeStruct(adjoint.shape,...  1.6 us

profile of v4, /device:TPU:0, one launch (start us, length us, event | category | flops | bytes accessed | tf_op | source)
XLA Modules:
  0.0 33.2 jit_solution(9882128227336145448)
XLA Ops:
  0.6 31.0 %shard_map.77 = (f32[3,8,16,128]{3,2,1,0:T(8,128)}, f32[1,32]{1,0:T(1,128)}) custom-call(f32[8,16,128]{2,1,0:T(8,128)} %bitcast.7, f32[2,8,16,128]{3,2,1,0:T(8,128)} %bitcast.6, f32[8,16,128]{2,1,0:T(8,128)} %bitcast.8, s32[4,2,128]{2,1,0:T(2,128)} %bitcast.9, s32[2,128]{1,0:T(2,128)} %zone_hbm.1, f32[32]{0:T(128)} %manning_hbm.1), custom_call_target="tpu_custom_call" | custom-call | tf_op jit(solution)/shard_map/pallas_call | solution.py:619
  31.6 1.6 %shard_map.78 = (f32[3,8,16,128]{3,2,1,0:T(8,128)}, f32[1,32]{1,0:T(1,128)}) custom-call(f32[3,8,16,128]{3,2,1,0:T(8,128)} %get-tuple-element.6.adjoint_ref, f32[1,32]{1,0:T(1,128)} %get-tuple-element.7.grad_ref), custom_call_target="tpu_custom_call" | custom-call | tf_op jit(solution)/shard_map/pallas_call | solution.py:674
